TPU v7x, 32 devices: a whole 2x2x4 slice. The times are simulated.
32 devices in a mesh: row: 4 (over y, x), col: 8 (over z, core).
Axes of the slice: x: 2, y: 2, z: 4, core: 2. Of those that a mesh axis runs over, the one named last changes fastest.
Arguments:
- hidden_in: bfloat16 [8192, 14336], P(('row', 'col')), may hold values from -6 to 6
- out_grad: bfloat16 [8192, 4096], P(('row', 'col')), may hold values from -6 to 6
- proj_in: bfloat16 [14336, 128], replicated, may hold values from -0.046875 to 0.046875
- proj_out: bfloat16 [4096, 128], replicated, may hold values from -0.09375 to 0.09375
- inverse_fisher: float32 [16384, 16384], P('row', 'col'), may hold values from -0.0625 to 0.0625
- queries: float32 [16384, 256], P('col'), may hold values from -6 to 6
- lengths: int32 [64], replicated, may hold values from 32 to 4352, as said below
- offsets: int32 [64], replicated, may hold values from 0 to 8191, as said below
Outputs:
- scores: float32 [64, 256], P(('row', 'col'))
Inputs may be any that keep to these rules, and one draw needn't show every extreme that they name: `lengths`: every sample has 32 tokens or more, and one sample has exactly 32; one sample has exactly half of all slots plus 256, and that is the most. Samples follow one another in slot order, each after 0 to 3 unused slots; slots after the last sample are unused; offsets[s] + lengths[s] <= 8192.
All inputs are finite; a program needn't handle non-finite values.
Results may differ from a plain program's by a relative error of at most 0.0003.
Values sent between devices are 32-bit elements; how exact they have to be, the bound alone decides.
No kernel may reach another device: no remote copies, remote signals or barrier semaphores. Data moves between devices by JAX's collectives and lax.ppermute only.
A program may use at most 128 MiB of HBM per device.

v0:
```python
import jax
import jax.numpy as jnp
from jax import lax
from jax.sharding import PartitionSpec as P

WINDOW = 9


score_scale = 0.0625


def exact_dot(left, right):
    return jnp.dot(left, right, precision=lax.Precision.HIGHEST, preferred_element_type=jnp.float32)


def body(hidden_in, out_grad, proj_in, proj_out, inverse_fisher, queries, lengths, offsets):
    tok_rows = hidden_in.shape[0]
    proj_tokens = jnp.dot(hidden_in, proj_in, preferred_element_type=jnp.float32)
    proj_grads = jnp.dot(out_grad, proj_out, preferred_element_type=jnp.float32)
    row_count = lax.axis_size("row")
    col_count = lax.axis_size("col")
    row_id = lax.axis_index("row")
    col_id = lax.axis_index("col")
    samples = lengths.shape[0]
    sample_ends = offsets + lengths

    def window_start(device):
        first_slot = device * tok_rows
        passed = jnp.sum((sample_ends <= first_slot).astype(jnp.int32))
        return jnp.minimum(passed, samples - WINDOW)

    device_id = row_id * col_count + col_id
    first_sample = window_start(device_id)
    win_offsets = lax.dynamic_slice_in_dim(offsets, first_sample, WINDOW, 0)
    win_ends = lax.dynamic_slice_in_dim(sample_ends, first_sample, WINDOW, 0)
    positions = device_id * tok_rows + jnp.arange(tok_rows, dtype=jnp.int32)
    member = (
        (positions[None, :] >= win_offsets[:, None]) & (positions[None, :] < win_ends[:, None])
    ).astype(jnp.float32)
    weighted = member[:, :, None] * proj_grads[None, :, :]
    window_grads = jnp.einsum(
        "wta,tb->wab", weighted, proj_tokens, precision=lax.Precision.HIGHEST
    ).reshape(WINDOW, -1)
    sample_axis = jnp.arange(samples, dtype=jnp.int32)
    u_block = lax.psum(exact_dot(inverse_fisher, queries), "col")
    received = lax.all_to_all(window_grads, "row", split_axis=1, concat_axis=0, tiled=True)
    partial_value = exact_dot(received, u_block)
    peer_ids = jnp.arange(row_count, dtype=jnp.int32) * col_count + col_id
    peer_first = jax.vmap(window_start)(peer_ids)
    targets = (peer_first[:, None] + jnp.arange(WINDOW, dtype=jnp.int32)[None, :]).reshape(-1)
    onehot = (sample_axis[:, None] == targets[None, :]).astype(jnp.float32)
    score_terms = exact_dot(onehot, partial_value)
    owned_scores = lax.psum_scatter(score_terms, ("row", "col"), scatter_dimension=0, tiled=True)
    owned_rows = owned_scores.shape[0]
    owned_lengths = lax.dynamic_slice_in_dim(lengths, device_id * owned_rows, owned_rows, 0)
    return score_scale * owned_scores / owned_lengths.astype(jnp.float32)[:, None]


def solution(mesh):
    in_specs = (
        P(("row", "col"), None),
        P(("row", "col"), None),
        P(),
        P(),
        P("row", "col"),
        P("col", None),
        P(),
        P(),
    )
    out_specs = P(("row", "col"), None)
    return jax.shard_map(body, mesh=mesh, in_specs=in_specs, out_specs=out_specs, check_vma=False)
```

profile of v0, /device:TPU:0, one launch (start us, length us, event | category | flops | bytes accessed | tf_op | source)
XLA Modules:
  0.0 269.9 jit_solution(15487176811788267068)
XLA Ops:
  6.5 0.0 copy-start
  6.5 0.0 all-reduce.4.cloned.1.call-start
  6.5 1.6 copy-done
  8.1 31.0 %fusion.9 = f32[4096,256]{1,0:T(8,128)} fusion(f32[4096,2048]{1,0:T(8,128)} %param.12, f32[2048,256]{1,0:T(8,128)S(1)} %copy-done), kind=kOutput, calls=%fused_computation.20 | convolution fusion | flops 25769803776 | bytes 39845888 | tf_op jit(solution)/shard_map/dot_general | solution.py:13
  39.2 0.0 copy-start.2
  39.2 0.0 copy-start.3
  39.2 0.0 copy-start.1
  39.2 0.0 all-reduce.4.cloned.1.call-update
  39.2 0.6 copy-done.2
  39.8 0.0 copy-done.3
  39.8 0.6 fusion.7
  41.1 0.1 dynamic_slice.9
  41.2 0.1 dynamic_slice.10
  41.3 0.1 and_convert_fusion
  41.3 0.0 copy-done.1
  41.3 2.4 fusion.8
  43.8 6.7 %convolution_bitcast_fusion = f32[256,128,1]{1,0,2:T(8,128)S(1)} fusion(bf16[256,14336]{1,0:T(8,128)(2,1)} %param.8, bf16[14336,128]{1,0:T(8,128)(2,1)} %param.10), kind=kOutput, calls=%fused_computation.2 | convolution fusion | flops 939524096 | bytes 11141120 | tf_op jit(solution)/shard_map/dot_general | solution.py:18
  50.4 1.1 fusion
  51.5 0.2 all_to_all.14
  51.7 1.4 copy.13
  53.1 5.2 %all-to-all-start = ((f32[9,4,4096]{2,0,1:T(8,128)}), f32[9,4,4096]{2,0,1:T(8,128)S(1)}, u32[]{:S(2)}, u32[]{:S(2)}) async-start(f32[9,4,4096]{2,0,1:T(8,128)} %copy.13), calls=%async_computation | async-start | bytes 2097152 | tf_op jit(solution)/shard_map/all_to_all | solution.py:46
  58.4 0.0 all-reduce.6.cloned.1.call-start
  58.4 0.2 convert_reduce_fusion
  58.6 0.1 iota_add_fusion
  58.6 0.1 add.63
  58.7 13.3 %all-to-all-done = f32[9,4,4096]{2,0,1:T(8,128)S(1)} async-done(((f32[9,4,4096]{2,0,1:T(8,128)}), f32[9,4,4096]{2,0,1:T(8,128)S(1)}, u32[]{:S(2)}, u32[]{:S(2)}) %all-to-all-start) | async-done | bytes 589856 | tf_op jit(solution)/shard_map/all_to_all | solution.py:46
  72.0 1.0 all_to_all.17
  73.0 65.6 %all-reduce.4.cloned.1.call-done = f32[4096,256]{1,0:T(8,128)} async-done(((f32[4096,256]{1,0:T(8,128)}), f32[4096,256]{1,0:T(8,128)}) %all-reduce.4.cloned.1.call-update) | async-done | bytes 4194320 | tf_op jit(solution)/shard_map/psum | solution.py:45
  138.6 4.5 %fusion.10 = f32[36,256]{1,0:T(8,128)S(1)} fusion(f32[36,4096]{1,0:T(8,128)} %all_to_all.17, f32[4096,256]{1,0:T(8,128)} %all-reduce.4.cloned.1.call-done), kind=kOutput, calls=%fused_computation.21 | convolution fusion | flops 452984832 | bytes 4820992 | tf_op jit(solution)/shard_map/dot_general | solution.py:13
  143.1 0.8 fusion.4
  143.9 0.0 all-reduce.6.cloned.1.call-update
  143.9 0.1 dynamic-slice_convert_fusion
  144.0 117.7 %all-reduce.6.cloned.1.call-done = f32[64,256]{1,0:T(8,128)} async-done(((f32[64,256]{1,0:T(8,128)}), f32[64,256]{1,0:T(8,128)}) %all-reduce.6.cloned.1.call-update) | async-done | bytes 65552
  261.7 1.3 fusion.6
  (3 shorter events, 0.0 us)
Async XLA Ops:
  6.5 1.6 copy-start
  6.5 132.0 %all-reduce.4.cloned.1.call-start = ((), (), s32[]{:S(2)}) async-start(), calls=%async_computation.1 | async-start | bytes 8388608 | tf_op jit(solution)/shard_map/psum | solution.py:45
  39.2 0.7 copy-start.2
  39.2 0.7 copy-start.3
  39.2 2.2 copy-start.1
  53.1 18.9 %all-to-all-start = ((f32[9,4,4096]{2,0,1:T(8,128)}), f32[9,4,4096]{2,0,1:T(8,128)S(1)}, u32[]{:S(2)}, u32[]{:S(2)}) async-start(f32[9,4,4096]{2,0,1:T(8,128)} %copy.13), calls=%async_computation | async-start | bytes 2097152 | tf_op jit(solution)/shard_map/all_to_all | solution.py:46
  58.4 203.4 %all-reduce.6.cloned.1.call-start = ((), (), s32[]{:S(2)}) async-start(), calls=%async_computation.2 | async-start | bytes 131072
Sparse Core Ops, SparseCore 0:
  39.3 99.2 all-reduce.3
  144.1 117.5 all-reduce.5
where the time goes:
time: 271 us; the launch traced here: 270 us
  waiting for transfers between devices  197 us (73%)
  matrix products  46.5 us (17%)
  between operations  14.1 us (5%)
  starting transfers between devices  5.24 us (2%)
  local copies, waits for them, and re-layouts  5.05 us (2%)
    unnamed x3, waiting for transfers between devices  118 us
    psum x1, waiting for transfers between devices, body(): u_block = lax.psum(exact_dot(inverse_fisher, queries), 'col')  65.6 us
    dot_general x3, matrix products, exact_dot(): jnp.dot(left, right, precision=lax.Precision.HIGHEST, preferred_element_t...  36.4 us
    all_to_all x1, waiting for transfers between devices, body(): lax.all_to_all(window_grads, 'row', split_axis=1, concat_axis=0, tiled=True)  13.3 us
    dot_general x1, matrix products, body(): jnp.dot(hidden_in, proj_in, preferred_element_type=jnp.float32)  6.65 us
  transfers between devices with their start and end apart: 3, of which 3 were waited for; matrix products, arithmetic and copies ran while one was open for 5% of the time, Pallas kernels for 0%

commit v1 on v0

v1 whole, which is shorter than its diff:
```python
import jax
import jax.numpy as jnp
from jax import lax
from jax.sharding import PartitionSpec as P

SHORTEST = 32
CORES = 2


score_scale = 0.0625


def near_dot(left, right):
    return jnp.dot(left, right, precision=lax.Precision.HIGH, preferred_element_type=jnp.float32)


def body(hidden_in, out_grad, proj_in, proj_out, inverse_fisher, queries, lengths, offsets):
    row_count = lax.axis_size("row")
    col_count = lax.axis_size("col")
    chip_count = col_count // CORES
    row_id = lax.axis_index("row")
    col_id = lax.axis_index("col")
    core_id = col_id % CORES
    chip_id = col_id // CORES
    device_id = row_id * col_count + col_id
    tok_rows = hidden_in.shape[0]
    rank = proj_out.shape[1]
    samples = lengths.shape[0]
    sample_ends = offsets + lengths
    window = min(samples, CORES * tok_rows // SHORTEST + 1)

    def other_core(x):
        return lax.ppermute(x, "col", [(i, i ^ 1) for i in range(col_count)])

    def along_row(x, step):
        return lax.ppermute(x, "row", [(i, i ^ step) for i in range(row_count)])

    def along_col(x, step):
        return lax.ppermute(x, "col", [(i, i ^ (CORES * step)) for i in range(col_count)])

    proj_grads = jnp.dot(out_grad, proj_out, preferred_element_type=jnp.float32)
    band = rank // row_count // CORES
    bands = proj_grads.reshape(tok_rows, row_count, CORES, band)
    grads_own = lax.dynamic_index_in_dim(bands, core_id, 2, False).reshape(tok_rows, row_count * band)
    grads_give = lax.dynamic_index_in_dim(bands, 1 - core_id, 2, False).reshape(tok_rows, row_count * band)
    proj_tokens = jnp.dot(hidden_in, proj_in, preferred_element_type=jnp.float32)
    grads_got = other_core(grads_give)
    tokens_got = other_core(proj_tokens)
    grads = jnp.concatenate([grads_own, grads_got])
    tokens = jnp.concatenate([proj_tokens, tokens_got])

    def window_start(chip):
        first_slot = chip * (CORES * tok_rows)
        passed = jnp.sum((sample_ends <= first_slot).astype(jnp.int32))
        return jnp.minimum(passed, samples - window)

    first_sample = window_start(device_id // CORES)
    win_offsets = lax.dynamic_slice_in_dim(offsets, first_sample, window, 0)
    win_ends = lax.dynamic_slice_in_dim(sample_ends, first_sample, window, 0)
    positions = jnp.concatenate(
        [d * tok_rows + jnp.arange(tok_rows, dtype=jnp.int32) for d in (device_id, device_id ^ 1)]
    )
    member = (
        (positions[None, :] >= win_offsets[:, None]) & (positions[None, :] < win_ends[:, None])
    ).astype(jnp.float32)
    weighted = member[:, None, :] * grads.T[None, :, :]
    wide = window * row_count * band
    window_grads = near_dot(weighted.reshape(wide, CORES * tok_rows), tokens)
    window_grads = window_grads.reshape(window, row_count, band * rank)

    sample_axis = jnp.arange(samples, dtype=jnp.int32)
    pieces, targets = [], []
    for step in range(row_count):
        peer = row_id ^ step
        piece = lax.dynamic_index_in_dim(window_grads, peer, 1, False)
        pieces.append(piece if step == 0 else along_row(piece, step))
        targets.append(window_start(peer * chip_count + chip_id) + jnp.arange(window, dtype=jnp.int32))
    onehot = (sample_axis[:, None] == jnp.concatenate(targets)[None, :]).astype(jnp.float32)
    sums = near_dot(onehot, jnp.concatenate(pieces))

    sums = sums.reshape(samples, chip_count, -1)
    own = lax.dynamic_index_in_dim(sums, chip_id, 1, False)
    for step in range(1, chip_count):
        own = own + along_col(lax.dynamic_index_in_dim(sums, chip_id ^ step, 1, False), step)
    parts = [own] + [along_col(own, step) for step in range(1, chip_count)]

    half = inverse_fisher.shape[0] // CORES
    give = near_dot(lax.dynamic_slice_in_dim(inverse_fisher, (1 - core_id) * half, half, 0), queries)
    got = other_core(give)
    keep = near_dot(lax.dynamic_slice_in_dim(inverse_fisher, core_id * half, half, 0), queries)
    product = (keep + got).reshape(chip_count, half // chip_count, -1)

    score_terms = jnp.zeros((samples, queries.shape[1]), jnp.float32)
    for step in range(chip_count):
        score_terms = score_terms + near_dot(parts[step], lax.dynamic_index_in_dim(product, chip_id ^ step, 0, False))

    everyone = ("row", "col")
    devices = row_count * col_count
    terms = lax.all_to_all(score_terms, everyone, split_axis=0, concat_axis=0, tiled=True)
    owned_rows = samples // devices
    owned_scores = jnp.sum(terms.reshape(devices, owned_rows, -1), axis=0)
    owned_lengths = lax.dynamic_slice_in_dim(lengths, device_id * owned_rows, owned_rows, 0)
    return score_scale * owned_scores / owned_lengths.astype(jnp.float32)[:, None]


def solution(mesh):
    in_specs = (
        P(("row", "col"), None),
        P(("row", "col"), None),
        P(),
        P(),
        P("row", "col"),
        P("col", None),
        P(),
        P(),
    )
    out_specs = P(("row", "col"), None)
    return jax.shard_map(body, mesh=mesh, in_specs=in_specs, out_specs=out_specs, check_vma=False)
```

time: 271 us -> 87.7 us (0.32)
  waiting for transfers between devices: 197 us -> 25.7 us
  starting transfers between devices: 5.24 us -> 18.1 us
  matrix products: 46.5 us -> 35 us
  between operations: 14.1 us -> 3.28 us
    unnamed x3 -> x0, waiting for transfers between devices: 118 us -> none
    psum x1 -> x0, waiting for transfers between devices: 65.6 us -> none  [body(): u_block = lax.psum(exact_dot(inverse_fisher, queries), 'col')]
    ppermute x0 -> x12, waiting for transfers between devices: none -> 18.4 us  [the longest x6 9.58 us: along_col(): lax.ppermute(x, 'col', [(i, i ^ CORES * step) for i in range(col_count)])]
    ppermute x0 -> x12, starting transfers between devices: none -> 14.3 us  [the longest x6 9.09 us: along_col(): lax.ppermute(x, 'col', [(i, i ^ CORES * step) for i in range(col_count)])]
    dot_general x4 -> x8, matrix products: 37.4 us -> 26 us  [near_dot(): jnp.dot(left, right, precision=lax.Precision.HIGH, preferred_element_type...]
    all_to_all x1, waiting for transfers between devices: 13.3 us -> 7.3 us  [body(): lax.all_to_all(score_terms, everyone, split_axis=0, concat_axis=0, tiled=...]
  transfers between devices with their start and end apart: 3 -> 13, of which waited for: 3 -> 5; matrix products, arithmetic and copies ran while one was open for 5% -> 41% of each run, Pallas kernels for 0% -> 0%
where the time goes in v1:
time: 87.7 us; the launch traced here: 87.4 us
  matrix products  35 us (40%)
  waiting for transfers between devices  25.7 us (29%)
  starting transfers between devices  18.1 us (21%)
  local copies, waits for them, and re-layouts  3.33 us (4%)
  between operations  3.28 us (4%)
  other arithmetic  1.98 us (2%)
    dot_general x8, matrix products, near_dot(): jnp.dot(left, right, precision=lax.Precision.HIGH, preferred_element_type...  26 us
    ppermute x6, waiting for transfers between devices, along_col(): lax.ppermute(x, 'col', [(i, i ^ CORES * step) for i in range(col_count)])  9.58 us
    ppermute x6, starting transfers between devices, along_col(): lax.ppermute(x, 'col', [(i, i ^ CORES * step) for i in range(col_count)])  9.09 us
    ppermute x3, waiting for transfers between devices, along_row(): return lax.ppermute(x, 'row', [(i, i ^ step) for i in range(row_count)])  8.85 us
    all_to_all x1, waiting for transfers between devices, body(): lax.all_to_all(score_terms, everyone, split_axis=0, concat_axis=0, tiled=...  7.3 us
    dot_general x1, matrix products, body(): jnp.dot(hidden_in, proj_in, preferred_element_type=jnp.float32)  6.18 us
    ppermute x3, starting transfers between devices, along_row(): return lax.ppermute(x, 'row', [(i, i ^ step) for i in range(row_count)])  4.17 us
    all_to_all x1, starting transfers between devices, body(): lax.all_to_all(score_terms, everyone, split_axis=0, concat_axis=0, tiled=...  3.76 us
  transfers between devices with their start and end apart: 13, of which 5 were waited for; matrix products, arithmetic and copies ran while one was open for 41% of the time, Pallas kernels for 0%

profile of v1, /device:TPU:0, one launch (start us, length us, event | category | flops | bytes accessed | tf_op | source)
XLA Modules:
  0.0 87.4 jit_solution(11984260988207035563)
XLA Ops:
  0.0 0.0 copy-start
  0.0 2.8 %fusion.48 = f32[256,128]{0,1:T(8,128)S(1)} fusion(bf16[256,4096]{1,0:T(8,128)(2,1)} %param.9, bf16[4096,128]{1,0:T(8,128)(2,1)} %param.11), kind=kOutput, calls=%fused_computation.84 | convolution fusion | flops 268435456 | bytes 3276800 | tf_op jit(solution)/shard_map/dot_general | solution.py:41
  2.9 0.5 collective-permute-start
  3.4 6.2 %fusion.49 = f32[256,128]{1,0:T(8,128)S(1)} fusion(bf16[256,14336]{1,0:T(8,128)(2,1)} %param.8, bf16[14336,128]{1,0:T(8,128)(2,1)} %param.10), kind=kOutput, calls=%fused_computation.85 | convolution fusion | flops 939524096 | bytes 11141120 | tf_op jit(solution)/shard_map/dot_general | solution.py:46
  9.6 0.1 collective-permute-start.1
  9.7 0.0 copy-done
  9.7 0.0 copy-start.1
  9.7 0.0 copy-start.2
  9.7 11.7 %fusion = f32[2048,256]{1,0:T(8,128)} fusion(f32[2048,256]{1,0:T(8,128)S(1)} %copy-done, f32[4096,2048]{1,0:T(8,128)} %param.12, s32[]{:T(128)S(6)} %select_n.80), kind=kOutput, calls=%fused_computation | convolution fusion | flops 6442450944 | bytes 20971524 | tf_op jit(solution)/shard_map/dot_general | solution.py:14
  21.4 0.5 collective-permute-start.8
  21.9 0.0 copy-done.1
  21.9 0.0 copy-done.2
  21.9 0.7 fusion.41
  23.2 0.1 dynamic_slice.61
  23.3 0.1 dynamic_slice.62
  23.4 0.1 and_convert_fusion
  25.9 0.0 collective-permute-done
  25.9 0.3 broadcast_multiply_fusion
  26.2 0.0 collective-permute-done.1
  26.2 1.0 %fusion.28 = f32[1088,128]{1,0:T(8,128)S(1)} fusion(f32[1088,512]{1,0:T(8,128)S(1)} %bitcast.57, f32[256,128]{1,0:T(8,128)S(1)} %collective-permute-done.1, f32[256,128]{1,0:T(8,128)S(1)} %fusion.49), kind=kOutput, calls=%fused_computation.28 | convolution fusion | flops 427884544 | bytes 3047424 | tf_op jit(solution)/shard_map/dot_general | solution.py:14
  27.3 0.2 reshape.80
  27.5 0.6 constant_dynamic-slice_fusion.7
  28.1 0.1 copy.27
  28.1 2.6 %collective-permute-start.2 = (f32[17,2048]{1,0:T(8,128)S(1)}, f32[17,2048]{1,0:T(8,128)S(1)}, u32[]{:S(2)}, u32[]{:S(2)}) collective-permute-start(f32[17,2048]{1,0:T(8,128)S(1)} %bitcast.65), channel_id=1, source_target_pairs={{0,8},{8,0},{16,24},{24,16},{1,9},{9,1},{17,25},{25,17},{2,10},{10... | collective-permute-start | bytes 417800 | tf_op jit(solution)/shard_map/ppermute | solution.py:36
  30.7 1.6 %collective-permute-start.3 = (f32[17,2048]{1,0:T(8,128)S(1)}, f32[17,2048]{1,0:T(8,128)S(1)}, u32[]{:S(2)}, u32[]{:S(2)}) collective-permute-start(f32[17,2048]{1,0:T(8,128)S(1)} %bitcast.66), channel_id=1, source_target_pairs={{0,16},{8,24},{16,0},{24,8},{1,17},{9,25},{17,1},{25,9},{2,18},{10... | collective-permute-start | bytes 417800 | tf_op jit(solution)/shard_map/ppermute | solution.py:36
  32.3 0.7 copy.25
  33.0 0.0 collective-permute-start.4
  33.1 0.1 pad_add_fusion.1
  33.2 3.3 %collective-permute-done.2 = f32[17,2048]{1,0:T(8,128)S(1)} collective-permute-done((f32[17,2048]{1,0:T(8,128)S(1)}, f32[17,2048]{1,0:T(8,128)S(1)}, u32[]{:S(2)}, u32[]{:S(2)}) %collective-permute-start.2) | collective-permute-done | bytes 139296 | tf_op jit(solution)/shard_map/ppermute | solution.py:36
  36.4 5.6 %collective-permute-done.3 = f32[17,2048]{1,0:T(8,128)S(1)} collective-permute-done((f32[17,2048]{1,0:T(8,128)S(1)}, f32[17,2048]{1,0:T(8,128)S(1)}, u32[]{:S(2)}, u32[]{:S(2)}) %collective-permute-start.3) | collective-permute-done | bytes 139296 | tf_op jit(solution)/shard_map/ppermute | solution.py:36
  42.0 0.0 collective-permute-done.4
  42.0 0.4 fusion.9
  42.4 0.4 reshape.81
  42.8 0.5 constant_dynamic-slice_fusion.3
  43.3 1.6 %collective-permute-start.5 = (f32[64,512]{1,0:T(8,128)S(1)}, f32[64,512]{1,0:T(8,128)S(1)}, u32[]{:S(2)}, u32[]{:S(2)}) collective-permute-start(f32[64,512]{1,0:T(8,128)S(1)} %bitcast.67), channel_id=1, source_target_pairs={{0,2},{1,3},{2,0},{3,1},{4,6},{5,7},{6,4},{7,5},{8,10},{9,11},{10,... | collective-permute-start | bytes 393224 | tf_op jit(solution)/shard_map/ppermute | solution.py:39
  44.9 2.7 %collective-permute-start.6 = (f32[64,512]{1,0:T(8,128)S(1)}, f32[64,512]{1,0:T(8,128)S(1)}, u32[]{:S(2)}, u32[]{:S(2)}) collective-permute-start(f32[64,512]{1,0:T(8,128)S(1)} %bitcast.68), channel_id=1, source_target_pairs={{0,4},{1,5},{2,6},{3,7},{4,0},{5,1},{6,2},{7,3},{8,12},{9,13},{10,... | collective-permute-start | bytes 393224 | tf_op jit(solution)/shard_map/ppermute | solution.py:39
  47.6 0.3 collective-permute-start.7
  47.9 1.9 %collective-permute-done.5 = f32[64,512]{1,0:T(8,128)S(1)} collective-permute-done((f32[64,512]{1,0:T(8,128)S(1)}, f32[64,512]{1,0:T(8,128)S(1)}, u32[]{:S(2)}, u32[]{:S(2)}) %collective-permute-start.5) | collective-permute-done | bytes 131104 | tf_op jit(solution)/shard_map/ppermute | solution.py:39
  49.7 7.7 %collective-permute-done.6 = f32[64,512]{1,0:T(8,128)S(1)} collective-permute-done((f32[64,512]{1,0:T(8,128)S(1)}, f32[64,512]{1,0:T(8,128)S(1)}, u32[]{:S(2)}, u32[]{:S(2)}) %collective-permute-start.6) | collective-permute-done | bytes 131104 | tf_op jit(solution)/shard_map/ppermute | solution.py:39
  57.4 0.0 collective-permute-done.7
  57.5 2.0 %collective-permute-start.9 = (f32[64,512]{1,0:T(8,128)S(1)}, f32[64,512]{1,0:T(8,128)S(1)}, u32[]{:S(2)}, u32[]{:S(2)}) collective-permute-start(f32[64,512]{1,0:T(8,128)S(1)} %fusion.33), channel_id=1, source_target_pairs={{0,2},{1,3},{2,0},{3,1},{4,6},{5,7},{6,4},{7,5},{8,10},{9,11},{10,... | collective-permute-start | bytes 393224 | tf_op jit(solution)/shard_map/ppermute | solution.py:39
  59.5 1.1 %collective-permute-start.10 = (f32[64,512]{1,0:T(8,128)S(1)}, f32[64,512]{1,0:T(8,128)S(1)}, u32[]{:S(2)}, u32[]{:S(2)}) collective-permute-start(f32[64,512]{1,0:T(8,128)S(1)} %fusion.33), channel_id=1, source_target_pairs={{0,4},{1,5},{2,6},{3,7},{4,0},{5,1},{6,2},{7,3},{8,12},{9,13},{10,... | collective-permute-start | bytes 393224 | tf_op jit(solution)/shard_map/ppermute | solution.py:39
  60.6 1.4 %collective-permute-start.11 = (f32[64,512]{1,0:T(8,128)S(1)}, f32[64,512]{1,0:T(8,128)S(1)}, u32[]{:S(2)}, u32[]{:S(2)}) collective-permute-start(f32[64,512]{1,0:T(8,128)S(1)} %fusion.33), channel_id=1, source_target_pairs={{0,6},{1,7},{2,4},{3,5},{4,2},{5,3},{6,0},{7,1},{8,14},{9,15},{10,... | collective-permute-start | bytes 393224 | tf_op jit(solution)/shard_map/ppermute | solution.py:39
  62.0 0.0 collective-permute-done.8
  62.0 11.7 %fusion.4 = f32[2048,256]{1,0:T(8,128)S(1)} fusion(f32[2048,256]{1,0:T(8,128)} %collective-permute-done.8, f32[2048,256]{1,0:T(8,128)S(1)} %copy-done, f32[4096,2048]{1,0:T(8,128)} %param.12, s32[]{:T(128)S(6)} %select_n.79), kind=kOutput, calls=%fused_computation.4 | convolution fusion | flops 6442975232 | bytes 23068676 | tf_op jit(solution)/shard_map/dot_general | solution.py:14
  73.7 0.0 collective-permute-done.9
  73.7 0.3 fusion.21
  74.0 0.0 collective-permute-done.10
  74.0 0.3 fusion.19
  74.3 0.0 collective-permute-done.11
  74.3 0.3 fusion.17
  74.6 0.3 fusion.8
  74.9 0.7 all_to_all.6
  75.6 3.8 %all-to-all-start = ((f32[32,2,256]{2,1,0:T(2,128)}), f32[32,2,256]{2,1,0:T(2,128)S(1)}, u32[]{:S(2)}, u32[]{:S(2)}) async-start(f32[32,2,256]{2,1,0:T(2,128)} %all_to_all.6), calls=%async_computation | async-start | bytes 131072 | tf_op jit(solution)/shard_map/all_to_all | solution.py:99
  79.4 0.1 dynamic-slice_convert_fusion
  79.4 7.3 %all-to-all-done = f32[32,2,256]{2,1,0:T(2,128)S(1)} async-done(((f32[32,2,256]{2,1,0:T(2,128)}), f32[32,2,256]{2,1,0:T(2,128)S(1)}, u32[]{:S(2)}, u32[]{:S(2)}) %all-to-all-start) | async-done | bytes 65568 | tf_op jit(solution)/shard_map/all_to_all | solution.py:99
  86.8 0.7 multiply_divide_fusion
  (13 shorter events, 0.3 us)
Async XLA Ops:
  0.0 9.7 %copy-start = (f32[2048,256]{1,0:T(8,128)S(1)}, f32[2048,256]{1,0:T(8,128)}, u32[]{:S(2)}) copy-start(f32[2048,256]{1,0:T(8,128)} %param.13) | copy-start | bytes 6291460
  2.9 23.0 %collective-permute-start = (f32[256,64]{0,1:T(8,128)S(1)}, f32[256,64]{0,1:T(8,128)S(1)}, u32[]{:S(2)}, u32[]{:S(2)}) collective-permute-start(f32[256,64]{0,1:T(8,128)S(1)} %bitcast.70), channel_id=1, source_target_pairs={{0,1},{1,0},{2,3},{3,2},{4,5},{5,4},{6,7},{7,6},{8,9},{9,8},{10,11... | collective-permute-start | bytes 196616 | tf_op jit(solution)/shard_map/ppermute | solution.py:33
  9.6 16.6 %collective-permute-start.1 = (f32[256,128]{1,0:T(8,128)S(1)}, f32[256,128]{1,0:T(8,128)S(1)}, u32[]{:S(2)}, u32[]{:S(2)}) collective-permute-start(f32[256,128]{1,0:T(8,128)S(1)} %fusion.49), channel_id=1, source_target_pairs={{0,1},{1,0},{2,3},{3,2},{4,5},{5,4},{6,7},{7,6},{8,9},{9,8},{10,11... | collective-permute-start | bytes 393224 | tf_op jit(solution)/shard_map/ppermute | solution.py:33
  9.7 12.2 %copy-start.1 = (s32[64]{0:T(128)S(1)}, s32[64]{0:T(128)}, u32[]{:S(2)}) copy-start(s32[64]{0:T(128)} %param.15) | copy-start | bytes 772
  9.7 12.2 %copy-start.2 = (s32[64]{0:T(128)S(1)}, s32[64]{0:T(128)}, u32[]{:S(2)}) copy-start(s32[64]{0:T(128)} %param.14) | copy-start | bytes 772
  21.4 40.6 %collective-permute-start.8 = (f32[2048,256]{1,0:T(8,128)}, f32[2048,256]{1,0:T(8,128)}, u32[]{:S(2)}, u32[]{:S(2)}) collective-permute-start(f32[2048,256]{1,0:T(8,128)} %fusion), channel_id=1, source_target_pairs={{0,1},{1,0},{2,3},{3,2},{4,5},{5,4},{6,7},{7,6},{8,9},{9,8},{10,11... | collective-permute-start | bytes 6291464 | tf_op jit(solution)/shard_map/ppermute | solution.py:33
  28.1 8.3 %collective-permute-start.2 = (f32[17,2048]{1,0:T(8,128)S(1)}, f32[17,2048]{1,0:T(8,128)S(1)}, u32[]{:S(2)}, u32[]{:S(2)}) collective-permute-start(f32[17,2048]{1,0:T(8,128)S(1)} %bitcast.65), channel_id=1, source_target_pairs={{0,8},{8,0},{16,24},{24,16},{1,9},{9,1},{17,25},{25,17},{2,10},{10... | collective-permute-start | bytes 417800 | tf_op jit(solution)/shard_map/ppermute | solution.py:36
  30.7 11.3 %collective-permute-start.3 = (f32[17,2048]{1,0:T(8,128)S(1)}, f32[17,2048]{1,0:T(8,128)S(1)}, u32[]{:S(2)}, u32[]{:S(2)}) collective-permute-start(f32[17,2048]{1,0:T(8,128)S(1)} %bitcast.66), channel_id=1, source_target_pairs={{0,16},{8,24},{16,0},{24,8},{1,17},{9,25},{17,1},{25,9},{2,18},{10... | collective-permute-start | bytes 417800 | tf_op jit(solution)/shard_map/ppermute | solution.py:36
  33.0 9.0 %collective-permute-start.4 = (f32[17,2048]{1,0:T(8,128)}, f32[17,2048]{1,0:T(8,128)S(1)}, u32[]{:S(2)}, u32[]{:S(2)}) collective-permute-start(f32[17,2048]{1,0:T(8,128)} %bitcast.50), channel_id=1, source_target_pairs={{0,24},{8,16},{16,8},{24,0},{1,25},{9,17},{17,9},{25,1},{2,26},{10... | collective-permute-start | bytes 417800 | tf_op jit(solution)/shard_map/ppermute | solution.py:36
  43.3 6.5 %collective-permute-start.5 = (f32[64,512]{1,0:T(8,128)S(1)}, f32[64,512]{1,0:T(8,128)S(1)}, u32[]{:S(2)}, u32[]{:S(2)}) collective-permute-start(f32[64,512]{1,0:T(8,128)S(1)} %bitcast.67), channel_id=1, source_target_pairs={{0,2},{1,3},{2,0},{3,1},{4,6},{5,7},{6,4},{7,5},{8,10},{9,11},{10,... | collective-permute-start | bytes 393224 | tf_op jit(solution)/shard_map/ppermute | solution.py:39
  44.9 12.5 %collective-permute-start.6 = (f32[64,512]{1,0:T(8,128)S(1)}, f32[64,512]{1,0:T(8,128)S(1)}, u32[]{:S(2)}, u32[]{:S(2)}) collective-permute-start(f32[64,512]{1,0:T(8,128)S(1)} %bitcast.68), channel_id=1, source_target_pairs={{0,4},{1,5},{2,6},{3,7},{4,0},{5,1},{6,2},{7,3},{8,12},{9,13},{10,... | collective-permute-start | bytes 393224 | tf_op jit(solution)/shard_map/ppermute | solution.py:39
  47.6 9.9 %collective-permute-start.7 = (f32[64,512]{1,0:T(8,128)S(1)}, f32[64,512]{1,0:T(8,128)S(1)}, u32[]{:S(2)}, u32[]{:S(2)}) collective-permute-start(f32[64,512]{1,0:T(8,128)S(1)} %bitcast.69), channel_id=1, source_target_pairs={{0,6},{1,7},{2,4},{3,5},{4,2},{5,3},{6,0},{7,1},{8,14},{9,15},{10,... | collective-permute-start | bytes 393224 | tf_op jit(solution)/shard_map/ppermute | solution.py:39
  57.5 16.2 %collective-permute-start.9 = (f32[64,512]{1,0:T(8,128)S(1)}, f32[64,512]{1,0:T(8,128)S(1)}, u32[]{:S(2)}, u32[]{:S(2)}) collective-permute-start(f32[64,512]{1,0:T(8,128)S(1)} %fusion.33), channel_id=1, source_target_pairs={{0,2},{1,3},{2,0},{3,1},{4,6},{5,7},{6,4},{7,5},{8,10},{9,11},{10,... | collective-permute-start | bytes 393224 | tf_op jit(solution)/shard_map/ppermute | solution.py:39
  59.5 14.5 %collective-permute-start.10 = (f32[64,512]{1,0:T(8,128)S(1)}, f32[64,512]{1,0:T(8,128)S(1)}, u32[]{:S(2)}, u32[]{:S(2)}) collective-permute-start(f32[64,512]{1,0:T(8,128)S(1)} %fusion.33), channel_id=1, source_target_pairs={{0,4},{1,5},{2,6},{3,7},{4,0},{5,1},{6,2},{7,3},{8,12},{9,13},{10,... | collective-permute-start | bytes 393224 | tf_op jit(solution)/shard_map/ppermute | solution.py:39
  60.6 13.7 %collective-permute-start.11 = (f32[64,512]{1,0:T(8,128)S(1)}, f32[64,512]{1,0:T(8,128)S(1)}, u32[]{:S(2)}, u32[]{:S(2)}) collective-permute-start(f32[64,512]{1,0:T(8,128)S(1)} %fusion.33), channel_id=1, source_target_pairs={{0,6},{1,7},{2,4},{3,5},{4,2},{5,3},{6,0},{7,1},{8,14},{9,15},{10,... | collective-permute-start | bytes 393224 | tf_op jit(solution)/shard_map/ppermute | solution.py:39
  75.6 11.2 %all-to-all-start = ((f32[32,2,256]{2,1,0:T(2,128)}), f32[32,2,256]{2,1,0:T(2,128)S(1)}, u32[]{:S(2)}, u32[]{:S(2)}) async-start(f32[32,2,256]{2,1,0:T(2,128)} %all_to_all.6), calls=%async_computation | async-start | bytes 131072 | tf_op jit(solution)/shard_map/all_to_all | solution.py:99

commit v2 on v0

v2 whole, which is shorter than its diff:
```python
import functools

import jax
import jax.numpy as jnp
from jax import lax
from jax.experimental import pallas as pl
from jax.experimental.pallas import tpu as pltpu
from jax.sharding import PartitionSpec as P

SHORTEST = 32
STEP = 256
SPLIT = 512
CORES = 2
VMEM = pl.BlockSpec(memory_space=pltpu.VMEM)
SMEM = pl.BlockSpec(memory_space=pltpu.SMEM)
ANY = pl.BlockSpec(memory_space=pl.ANY)
HBM = pl.BlockSpec(memory_space=pltpu.HBM)

score_scale = 0.0625


def halves(x):
    high = x.astype(jnp.bfloat16)
    low = (x - high.astype(jnp.float32)).astype(jnp.bfloat16)
    return high, low


def dot(left, right):
    return jnp.dot(left, right, preferred_element_type=jnp.float32)


def params(mib):
    return pltpu.CompilerParams(vmem_limit_bytes=mib * 2**20)


def project_kernel(steps, row_count, place, hidden, grad, proj_in, proj_out, own, give, *scratch):
    hidden_v, grad_v, in_v, out_v, sems = scratch
    jobs = []
    for source, weights, left, right, count in (
        (grad, proj_out, grad_v, out_v, steps[0]),
        (hidden, proj_in, hidden_v, in_v, steps[1]),
    ):
        wide = source.shape[1] // count
        job = []
        for i in range(count):
            span = pl.ds(i * wide, wide)
            slot = len(jobs) * steps[0] + i
            a = pltpu.make_async_copy(source.at[:, span], left.at[:, span], sems.at[0, slot])
            b = pltpu.make_async_copy(weights.at[span, :], right.at[span, :], sems.at[1, slot])
            a.start()
            b.start()
            job.append((span, a, b))
        jobs.append((left, right, job))
    results = []
    for left, right, job in jobs:
        total = None
        for span, a, b in job:
            a.wait()
            b.wait()
            term = dot(left[:, span], right[span, :])
            total = term if total is None else total + term
        results.append(total)
    grads, tokens = results
    tok_rows, rank = tokens.shape
    band = rank // row_count // CORES
    turned = grads.T.reshape(row_count, CORES, band, tok_rows)
    first = turned[:, 0].reshape(row_count * band, tok_rows)
    second = turned[:, 1].reshape(row_count * band, tok_rows)
    mine = place[1] % CORES == 0
    tall = row_count * band
    for ref, value in ((own, jnp.where(mine, first, second)), (give, jnp.where(mine, second, first))):
        for i in range(tok_rows // rank):
            ref[i * tall : (i + 1) * tall, :] = value[:, i * rank : (i + 1) * rank]
        ref[tok_rows // rank * tall :, :] = tokens


def project(place, hidden_in, out_grad, proj_in, proj_out, row_count):
    tok_rows, rank = hidden_in.shape[0], proj_in.shape[1]
    steps = (2, 7)
    tall = tok_rows // rank * (rank // CORES) + tok_rows
    out = jax.ShapeDtypeStruct((tall, rank), jnp.float32)
    return pl.pallas_call(
        functools.partial(project_kernel, steps, row_count),
        out_shape=(out, out),
        in_specs=[SMEM, HBM, HBM, HBM, HBM],
        out_specs=(VMEM, VMEM),
        scratch_shapes=[
            pltpu.VMEM(hidden_in.shape, hidden_in.dtype),
            pltpu.VMEM(out_grad.shape, out_grad.dtype),
            pltpu.VMEM(proj_in.shape, proj_in.dtype),
            pltpu.VMEM(proj_out.shape, proj_out.dtype),
            pltpu.SemaphoreType.DMA((2, sum(steps))),
        ],
        compiler_params=params(53),
        name="project",
    )(place, hidden_in, out_grad, proj_in, proj_out)


def first_of_window(ends, first_slot, samples, window):
    passed = jnp.sum((ends[...] <= first_slot).astype(jnp.int32))
    return jnp.minimum(passed, samples - window)


def window_kernel(window, sizes, tok_rows, place, offsets, lengths, ends, own, got, *refs):
    row_count, col_count = sizes
    outs, left = refs[:row_count], refs[row_count]
    device = place[0] * col_count + place[1]
    first_sample = first_of_window(ends, device // CORES * (CORES * tok_rows), lengths.shape[0], window)
    rank = own.shape[1]
    strips = tok_rows // rank
    tall = (own.shape[0] - tok_rows) // strips
    pieces = [ref[i * tall : (i + 1) * tall, :] for ref in (own, got) for i in range(strips)]
    grads_high, grads_low = halves(jnp.concatenate(pieces, axis=1))
    high, low = halves(jnp.concatenate([own[strips * tall :, :], got[strips * tall :, :]], axis=0))
    tokens = jnp.concatenate([high, low], axis=1)
    lanes = lax.broadcasted_iota(jnp.int32, (1, 2 * tok_rows), 1)
    other = device + 1 - 2 * (place[1] % CORES)
    positions = jnp.where(lanes < tok_rows, device * tok_rows + lanes, (other - 1) * tok_rows + lanes)
    both = jnp.concatenate([grads_high, grads_low], axis=0)
    for w in range(window):
        begin = offsets[first_sample + w]
        inside = (positions >= begin) & (positions < begin + lengths[first_sample + w])
        left[w * 2 * tall : (w + 1) * 2 * tall, :] = both * inside.astype(jnp.bfloat16)
    sums = dot(left[...], tokens)
    band = tall // row_count
    sums = sums.reshape(window, 2, row_count, band, 2 * rank)
    sums = sums[:, 0, :, :, :rank] + (sums[:, 0, :, :, rank:] + sums[:, 1, :, :, :rank])
    for r in range(row_count):
        step = place[0] ^ r
        for s in range(row_count):

            @pl.when(step == s)
            def _():
                outs[s][...] = sums[:, r]


def windows(place, offsets, lengths, ends, own, got, window, sizes, tok_rows):
    rank = own.shape[1]
    tall = (own.shape[0] - tok_rows) // (tok_rows // rank)
    out = jax.ShapeDtypeStruct((window, tall // sizes[0], rank), jnp.float32)
    return pl.pallas_call(
        functools.partial(window_kernel, window, sizes, tok_rows),
        out_shape=(out,) * sizes[0],
        in_specs=[SMEM, SMEM, SMEM, VMEM, VMEM, VMEM],
        out_specs=(VMEM,) * sizes[0],
        scratch_shapes=[pltpu.VMEM((window * 2 * tall, 2 * tok_rows), jnp.bfloat16)],
        compiler_params=params(40),
        cost_estimate=pl.CostEstimate(
            flops=16 * window * tall * tok_rows * rank, bytes_accessed=8 * window * tall * rank, transcendentals=0
        ),
        name="windows",
    )(place, offsets, lengths, ends, own, got)


def spread_kernel(sizes, tok_rows, place, ends, *refs):
    row_count, col_count = sizes
    pieces, outs, total = refs[:row_count], refs[row_count + 1 : -1], refs[-1]
    total[...] = jnp.zeros_like(total)
    window = pieces[0].shape[0]
    chip = place[1] // CORES
    for d in range(row_count):
        source = (place[0] ^ d) * (col_count // CORES) + chip
        first = first_of_window(ends, source * (CORES * tok_rows), total.shape[0], window)
        span = pl.ds(first, window)
        total[span] = total[span] + pieces[d][...]
    count = outs[0].shape[0]
    for d, out in enumerate(outs):
        out[...] = total[pl.ds((chip ^ d) * count, count)]


def spread(place, ends, pieces, after, samples, sizes, tok_rows):
    tail = pieces[0].shape[1:]
    chip_count = sizes[1] // CORES
    out = jax.ShapeDtypeStruct((samples // chip_count, *tail), jnp.float32)
    return pl.pallas_call(
        functools.partial(spread_kernel, sizes, tok_rows),
        out_shape=(out,) * chip_count,
        in_specs=[SMEM, VMEM] + [VMEM] * len(pieces) + [ANY],
        out_specs=(VMEM,) * chip_count,
        scratch_shapes=[pltpu.VMEM((samples, *tail), jnp.float32)],
        compiler_params=params(40),
        name="spread",
    )(place, ends, *pieces, after)


def sum_kernel(after, through, *refs):
    total = refs[0][...]
    for ref in refs[1:-2]:
        total = total + ref[...]
    refs[-2][...] = total


def sum_of(parts, after, through):
    return pl.pallas_call(
        sum_kernel,
        out_shape=(
            jax.ShapeDtypeStruct(parts[0].shape, jnp.float32),
            jax.ShapeDtypeStruct(through.shape, through.dtype),
        ),
        in_specs=[ANY, ANY] + [VMEM] * len(parts),
        out_specs=(VMEM, ANY),
        input_output_aliases={1: 1},
        compiler_params=params(40),
        name="sum_parts",
    )(after, through, *parts)


def across(left, right):
    return lax.dot_general(left, right, (((1,), (1,)), ((), ())), preferred_element_type=jnp.float32)


def product_kernel(chunks, turn, half, place, after, fisher, queries, *refs):
    count = len(chunks) + (1 if turn else 0)
    outs, scratch = refs[:count], refs[count:]
    fisher_v, split, sems = scratch[:3]
    core = place[1] % CORES
    if turn:
        start = pltpu.make_async_copy(queries, scratch[3], sems.at[0])
        start.start()
    copies, at = [], 0
    for ours, first, rows in chunks:
        source = jnp.where(core == 0, first, half + first) if ours else jnp.where(core == 0, half + first, first)
        source = pl.multiple_of(source, STEP)
        for step in range(0, rows, STEP):
            copy = pltpu.make_async_copy(
                fisher.at[pl.ds(source + step, STEP), :],
                fisher_v.at[pl.ds(at, STEP), :],
                sems.at[1 + at // STEP],
            )
            copy.start()
            copies.append(copy)
            at += STEP
    if turn:
        start.wait()
        high, low = halves(scratch[3][...].T)
        width = high.shape[0]
        outs[0][:width, :] = high
        outs[0][width:, :] = low
        turned, outs = outs[0], outs[1:]
    else:
        turned = queries
        width = turned.shape[0] // 2
    at = 0
    for out, (_, _, rows) in zip(outs, chunks):
        for begin in range(0, rows, SPLIT):
            size = min(SPLIT, rows - begin)
            for step in range(0, size, STEP):
                copies[at // STEP].wait()
                split[0, step : step + STEP, :], split[1, step : step + STEP, :] = halves(fisher_v[at : at + STEP, :])
                at += STEP
            term = across(turned[...], split[0, :size, :])
            term = term[:width] + (term[width:] + across(turned[:width, :], split[1, :size, :]))
            out[:, begin : begin + size] = term


def product(place, after, inverse_fisher, queries, chunks, turn=False):
    width = queries.shape[1] if turn else queries.shape[0] // 2
    depth = inverse_fisher.shape[1]
    out_shape = [jax.ShapeDtypeStruct((2 * width, depth), jnp.bfloat16)] if turn else []
    out_shape += [jax.ShapeDtypeStruct((width, chunk[2]), jnp.float32) for chunk in chunks]
    rows = sum(chunk[2] for chunk in chunks)
    half = inverse_fisher.shape[0] // CORES
    return pl.pallas_call(
        functools.partial(product_kernel, chunks, turn, half),
        out_shape=tuple(out_shape),
        in_specs=[SMEM, ANY, HBM, ANY if turn else VMEM],
        out_specs=(VMEM,) * len(out_shape),
        scratch_shapes=[
            pltpu.VMEM((rows, depth), jnp.float32),
            pltpu.VMEM((2, min(SPLIT, max(chunk[2] for chunk in chunks)), depth), jnp.bfloat16),
            pltpu.SemaphoreType.DMA((1 + rows // STEP,)),
        ]
        + ([pltpu.VMEM(queries.shape, queries.dtype)] if turn else []),
        compiler_params=params(36),
        cost_estimate=pl.CostEstimate(
            flops=6 * rows * depth * width, bytes_accessed=4 * rows * depth, transcendentals=0
        ),
        name="product",
    )(place, after, inverse_fisher, queries)


def merge(keeps, gots):
    shape = (keeps[0].shape[0], sum(keep.shape[1] for keep in keeps))

    def kernel(*refs):
        ins, (high, low) = refs[:-2], refs[-2:]
        left = [(ref, at) for ref in ins[: len(keeps)] for at in range(0, ref.shape[1], STEP)]
        right = [(ref, at) for ref in ins[len(keeps) :] for at in range(0, ref.shape[1], STEP)]
        for i, ((a, at), (b, to)) in enumerate(zip(left, right)):
            span = slice(i * STEP, (i + 1) * STEP)
            high[:, span], low[:, span] = halves(a[:, at : at + STEP] + b[:, to : to + STEP])

    out = jax.ShapeDtypeStruct(shape, jnp.bfloat16)
    return pl.pallas_call(
        kernel,
        out_shape=(out, out),
        in_specs=[VMEM] * (len(keeps) + len(gots)),
        out_specs=(VMEM, VMEM),
        compiler_params=params(36),
        name="merge",
    )(*keeps, *gots)


def score_kernel(chip_count, pieces, band, place, *refs):
    parts, high, low = refs[:chip_count], refs[chip_count : chip_count + pieces], refs[chip_count + pieces : -2]
    out, left = refs[-2:]
    count = parts[0].shape[0] // band
    rank = parts[0].shape[1]
    chip = place[1] // CORES
    for d, part in enumerate(parts):
        rows = pl.ds(pl.multiple_of((chip ^ d) * count, count), count)
        for a in range(band):
            left[rows, a * rank : (a + 1) * rank] = part[pl.ds(a, count, stride=band), :]
    left_high, left_low = halves(left[...])
    samples = left_high.shape[0]
    both = jnp.concatenate([left_high, left_low], axis=0)
    total, at = None, 0
    for p in range(pieces):
        depth = high[p].shape[1]
        span = slice(at, at + depth)
        term = across(both[:, span], high[p][...])
        term = term[:samples] + (term[samples:] + across(left_high[:, span], low[p][...]))
        total = term if total is None else total + term
        at += depth
    out[...] = total.reshape(out.shape)


def score(place, parts, high, low, samples, devices, band):
    rank = parts[0].shape[1]
    width = high[0].shape[0]
    return pl.pallas_call(
        functools.partial(score_kernel, len(parts), len(high), band),
        out_shape=jax.ShapeDtypeStruct((devices, samples // devices, width), jnp.float32),
        in_specs=[SMEM] + [VMEM] * (len(parts) + len(high) + len(low)),
        out_specs=VMEM,
        scratch_shapes=[pltpu.VMEM((samples, band * rank), jnp.float32)],
        compiler_params=params(40),
        name="score",
    )(place, *parts, *high, *low)


def body(hidden_in, out_grad, proj_in, proj_out, inverse_fisher, queries, lengths, offsets):
    row_count = lax.axis_size("row")
    col_count = lax.axis_size("col")
    sizes = (row_count, col_count)
    chip_count = col_count // CORES
    row_id = lax.axis_index("row")
    col_id = lax.axis_index("col")
    tok_rows = hidden_in.shape[0]
    rank = proj_out.shape[1]
    samples = lengths.shape[0]
    ends = (offsets + lengths)[None, :]
    window = min(samples, CORES * tok_rows // SHORTEST + 1)
    band = rank // row_count // CORES
    place = jnp.stack([row_id, col_id])

    def other_core(x):
        return lax.ppermute(x, "col", [(i, i ^ 1) for i in range(col_count)])

    def along_row(x, step):
        return lax.ppermute(x, "row", [(i, i ^ step) for i in range(row_count)])

    def along_col(x, step):
        return lax.ppermute(x, "col", [(i, i ^ (CORES * step)) for i in range(col_count)])

    own, give = project(place, hidden_in, out_grad, proj_in, proj_out, row_count)
    got = other_core(give)
    pieces = windows(place, offsets, lengths, ends, own, got, window, sizes, tok_rows)

    half = inverse_fisher.shape[0] // CORES
    mid, quarter = half // 2, half // 4
    arrived = [pieces[0]] + [along_row(pieces[d], d) for d in reversed(range(1, row_count))][::-1]
    turned, give_a = product(place, pieces[0], inverse_fisher, queries, [(False, 0, mid)], turn=True)
    chunks = spread(place, ends, arrived, give_a, samples, sizes, tok_rows)

    arrived = [chunks[0]] + [along_col(chunks[d], d) for d in reversed(range(1, chip_count))][::-1]
    give_b, keep_a = product(place, chunks[0], inverse_fisher, turned, [(False, mid, mid), (True, 0, quarter)])
    total, give_b = sum_of(arrived[::-1], keep_a, give_b)

    parts = [total] + [along_col(total, d) for d in reversed(range(1, chip_count))][::-1]
    (keep_b,) = product(place, total, inverse_fisher, turned, [(True, quarter, half - quarter)])
    high, low = merge([keep_a, keep_b], [other_core(give_a), other_core(give_b)])
    parts = [part.reshape(-1, rank) for part in parts]
    devices = row_count * col_count
    score_terms = score(place, parts, [high], [low], samples, devices, band)

    terms = lax.all_to_all(score_terms, ("row", "col"), split_axis=0, concat_axis=0, tiled=True)
    owned_rows = samples // devices
    owned_scores = jnp.sum(terms, axis=0)
    device_id = row_id * col_count + col_id
    owned_lengths = lax.dynamic_slice_in_dim(lengths, device_id * owned_rows, owned_rows, 0)
    return score_scale * owned_scores / owned_lengths.astype(jnp.float32)[:, None]


def solution(mesh):
    in_specs = (
        P(("row", "col"), None),
        P(("row", "col"), None),
        P(),
        P(),
        P("row", "col"),
        P("col", None),
        P(),
        P(),
    )
    out_specs = P(("row", "col"), None)
    return jax.shard_map(body, mesh=mesh, in_specs=in_specs, out_specs=out_specs, check_vma=False)
```

time: 271 us -> 67.4 us (0.25)
  waiting for transfers between devices: 197 us -> 10.4 us
  matrix products: 46.5 us -> 0 us
  Pallas kernels: 0 us -> 36.5 us
  starting transfers between devices: 5.24 us -> 19.2 us
  between operations: 14.1 us -> 0.19 us
  local copies, waits for them, and re-layouts: 5.05 us -> 0.01 us
    unnamed x3 -> x0, waiting for transfers between devices: 118 us -> none
    psum x1 -> x0, waiting for transfers between devices: 65.6 us -> none  [body(): u_block = lax.psum(exact_dot(inverse_fisher, queries), 'col')]
    dot_general x6 -> x0, matrix products: 46.5 us -> none  [the longest x3 36.4 us: exact_dot(): jnp.dot(left, right, precision=lax.Precision.HIGHEST, preferred_element_t...]
    pallas_call x0 -> x9, Pallas kernels: none -> 36.5 us  [the longest x3 25.4 us: product(): pl.pallas_call(functools.partial(product_kernel, chunks, turn, half), out...]
    ppermute x0 -> x12, starting transfers between devices: none -> 14.3 us  [the longest x6 9.2 us: along_col(): lax.ppermute(x, 'col', [(i, i ^ CORES * step) for i in range(col_count)])]
    all_to_all x1, waiting for transfers between devices: 13.3 us -> 7.3 us  [body(): lax.all_to_all(score_terms, ('row', 'col'), split_axis=0, concat_axis=0,...]
    ppermute x0 -> x12, waiting for transfers between devices: none -> 3.12 us  [the longest x6 2.04 us: along_col(): lax.ppermute(x, 'col', [(i, i ^ CORES * step) for i in range(col_count)])]
  transfers between devices with their start and end apart: 3 -> 13, of which waited for: 3 -> 3; matrix products, arithmetic and copies ran while one was open for 5% -> 0% of each run, Pallas kernels for 0% -> 40%
where the time goes in v2:
time: 67.4 us; the launch traced here: 67.2 us
  Pallas kernels  36.5 us (54%)
  starting transfers between devices  19.2 us (28%)
  waiting for transfers between devices  10.4 us (15%)
  other arithmetic  0.85 us (1%)
    pallas_call x3, Pallas kernels, product(): pl.pallas_call(functools.partial(product_kernel, chunks, turn, half), out...  25.4 us
    ppermute x6, starting transfers between devices, along_col(): lax.ppermute(x, 'col', [(i, i ^ CORES * step) for i in range(col_count)])  9.2 us
    all_to_all x1, waiting for transfers between devices, body(): lax.all_to_all(score_terms, ('row', 'col'), split_axis=0, concat_axis=0,...  7.3 us
    pallas_call x1, Pallas kernels, project(): pl.pallas_call(functools.partial(project_kernel, steps, row_count), out_s...  6.3 us
    all_to_all x1, starting transfers between devices, body(): lax.all_to_all(score_terms, ('row', 'col'), split_axis=0, concat_axis=0,...  4.9 us
    ppermute x3, starting transfers between devices, along_row(): return lax.ppermute(x, 'row', [(i, i ^ step) for i in range(row_count)])  4.46 us
    pallas_call x1, Pallas kernels, score(): pl.pallas_call(functools.partial(score_kernel, len(parts), len(high), ban...  2.07 us
    ppermute x6, waiting for transfers between devices, along_col(): lax.ppermute(x, 'col', [(i, i ^ CORES * step) for i in range(col_count)])  2.04 us
  transfers between devices with their start and end apart: 13, of which 3 were waited for; matrix products, arithmetic and copies ran while one was open for 0% of the time, Pallas kernels for 40%

profile of v2, /device:TPU:0, one launch (start us, length us, event | category | flops | bytes accessed | tf_op | source)
XLA Modules:
  0.0 67.2 jit_solution(13314772894329449359)
XLA Ops:
  0.0 0.1 pad_add_fusion.place
  0.1 0.0 copy-start.1
  0.1 0.0 copy-start.2
  0.1 6.3 %project.1 = (f32[384,128]{1,0:T(8,128)S(1)}, f32[384,128]{1,0:T(8,128)S(1)}) custom-call(s32[2]{0:T(128)S(1)} %pad_add_fusion.place, bf16[256,14336]{1,0:T(8,128)(2,1)} %hidden.1, bf16[256,4096]{1,0:T(8,128)(2,1)} %grad.1, bf16[14336,128]{1,0:T(8,128)(2,1)} %proj_in.1, bf16[4096,128]{1,0:T(8,128)(2,1)} %proj_out.1), custom_call_target="tpu_custom_call" | custom-call | tf_op jit(solution)/shard_map/project/pallas_call | solution.py:82
  6.4 0.0 copy-start
  6.4 0.5 collective-permute-start
  6.9 0.0 copy-done.1
  6.9 0.0 copy-done.2
  6.9 1.1 %collective-permute-done.got = f32[384,128]{1,0:T(8,128)S(1)} collective-permute-done((f32[384,128]{1,0:T(8,128)S(1)}, f32[384,128]{1,0:T(8,128)S(1)}, u32[]{:S(2)}, u32[]{:S(2)}) %collective-permute-start) | collective-permute-done | bytes 196640 | tf_op jit(solution)/shard_map/ppermute | solution.py:358
  8.0 1.5 %windows.1 = (f32[17,16,128]{2,1,0:T(8,128)S(1)}, f32[17,16,128]{2,1,0:T(8,128)S(1)}, f32[17,16,128]{2,1,0:T(8,128)S(1)}, f32[17,16,128]{2,1,0:T(8,128)S(1)}) custom-call(s32[2]{0:T(128)S(1)} %pad_add_fusion.place, s32[64]{0:T(128)S(1)} %copy-done.1, s32[64]{0:T(128)S(1)} %copy-done.2, s32[1,64]{1,0:T(1,128)S(1)} %add_bitcast_fusion.ends, ...), custom_call_target="tpu_custom_call" | custom-call | flops 570425344 | bytes 1114112 | tf_op jit(solution)/shard_map/windows/pallas_call | solution.py:141
  9.5 2.9 %collective-permute-start.1 = (f32[17,16,128]{2,1,0:T(8,128)S(1)}, f32[17,16,128]{2,1,0:T(8,128)S(1)}, u32[]{:S(2)}, u32[]{:S(2)}) collective-permute-start(f32[17,16,128]{2,1,0:T(8,128)S(1)} %get-tuple-element.26), channel_id=1, source_target_pairs={{0,8},{8,0},{16,24},{24,16},{1,9},{9,1},{17,25},{25,17},{2,10},{10... | collective-permute-start | bytes 417800 | tf_op jit(solution)/shard_map/ppermute | solution.py:361
  12.4 1.5 %collective-permute-start.2 = (f32[17,16,128]{2,1,0:T(8,128)S(1)}, f32[17,16,128]{2,1,0:T(8,128)S(1)}, u32[]{:S(2)}, u32[]{:S(2)}) collective-permute-start(f32[17,16,128]{2,1,0:T(8,128)S(1)} %get-tuple-element.27), channel_id=1, source_target_pairs={{0,16},{8,24},{16,0},{24,8},{1,17},{9,25},{17,1},{25,9},{2,18},{10... | collective-permute-start | bytes 417800 | tf_op jit(solution)/shard_map/ppermute | solution.py:361
  13.9 0.0 collective-permute-start.3
  14.0 0.0 copy-done
  14.0 7.2 %product.3 = (bf16[512,2048]{1,0:T(8,128)(2,1)S(1)}, f32[256,1024]{1,0:T(8,128)S(1)}) custom-call(s32[2]{0:T(128)S(1)} %pad_add_fusion.place, f32[17,16,128]{2,1,0:T(8,128)S(1)} %get-tuple-element.25.after.refs_0_, f32[4096,2048]{1,0:T(8,128)} %fisher.5, f32[2048,256]{1,0:T(8,128)S(1)} %copy-done), custom_call_target="tpu_custom_call" | custom-call | flops 3221225472 | bytes 8388608 | tf_op jit(solution)/shard_map/product/pallas_call | solution.py:263
  21.1 0.1 collective-permute-start.10
  21.2 0.0 collective-permute-done.1.refs_1_
  21.2 0.0 collective-permute-done.2.refs_2_
  21.2 0.0 collective-permute-done.3.refs_3_
  21.2 0.8 %spread.1 = (f32[16,16,128]{2,1,0:T(8,128)S(1)}, f32[16,16,128]{2,1,0:T(8,128)S(1)}, f32[16,16,128]{2,1,0:T(8,128)S(1)}, f32[16,16,128]{2,1,0:T(8,128)S(1)}) custom-call(s32[2]{0:T(128)S(1)} %pad_add_fusion.place, s32[1,64]{1,0:T(1,128)S(1)} %add_bitcast_fusion.ends, f32[17,16,128]{2,1,0:T(8,128)S(1)} %get-tuple-element.25.after.refs_0_, ...), custom_call_target="tpu_custom_call" | custom-call | tf_op jit(solution)/shard_map/spread/pallas_call | solution.py:175
  22.0 4.1 %collective-permute-start.4 = (f32[16,16,128]{2,1,0:T(8,128)S(1)}, f32[16,16,128]{2,1,0:T(8,128)S(1)}, u32[]{:S(2)}, u32[]{:S(2)}) collective-permute-start(f32[16,16,128]{2,1,0:T(8,128)S(1)} %get-tuple-element.34), channel_id=1, source_target_pairs={{0,6},{1,7},{2,4},{3,5},{4,2},{5,3},{6,0},{7,1},{8,14},{9,15},{10,... | collective-permute-start | bytes 393224 | tf_op jit(solution)/shard_map/ppermute | solution.py:364
  26.1 0.0 collective-permute-start.5
  26.1 0.6 collective-permute-start.6
  26.8 9.0 %product.4 = (f32[256,1024]{1,0:T(8,128)S(1)}, f32[256,512]{1,0:T(8,128)S(1)}) custom-call(s32[2]{0:T(128)S(1)} %pad_add_fusion.place, f32[16,16,128]{2,1,0:T(8,128)S(1)} %get-tuple-element.30.after.refs_3_, f32[4096,2048]{1,0:T(8,128)} %fisher.5, bf16[512,2048]{1,0:T(8,128)(2,1)S(1)} %get-tuple-element.31.queries), custom_call_target="tpu_custom_call" | custom-call | flops 4831838208 | bytes 12582912 | tf_op jit(solution)/shard_map/product/pallas_call | solution.py:263
  35.8 0.0 collective-permute-done.4.refs_0_
  35.8 2.0 %collective-permute-done.5.refs_1_ = f32[16,16,128]{2,1,0:T(8,128)S(1)} collective-permute-done((f32[16,16,128]{2,1,0:T(8,128)S(1)}, f32[16,16,128]{2,1,0:T(8,128)S(1)}, u32[]{:S(2)}, u32[]{:S(2)}) %collective-permute-start.5) | collective-permute-done | bytes 131104 | tf_op jit(solution)/shard_map/ppermute | solution.py:364
  37.8 0.0 collective-permute-done.6.refs_2_
  37.9 0.1 collective-permute-start.11
  38.0 0.1 collective-permute-start.7
  38.0 3.0 %collective-permute-start.8 = (f32[16,16,128]{2,1,0:T(8,128)S(1)}, f32[16,16,128]{2,1,0:T(8,128)S(1)}, u32[]{:S(2)}, u32[]{:S(2)}) collective-permute-start(f32[16,16,128]{2,1,0:T(8,128)S(1)} %get-tuple-element.37.after), channel_id=1, source_target_pairs={{0,4},{1,5},{2,6},{3,7},{4,0},{5,1},{6,2},{7,3},{8,12},{9,13},{10,... | collective-permute-start | bytes 393224 | tf_op jit(solution)/shard_map/ppermute | solution.py:364
  41.1 1.3 %collective-permute-start.9 = (f32[16,16,128]{2,1,0:T(8,128)S(1)}, f32[16,16,128]{2,1,0:T(8,128)S(1)}, u32[]{:S(2)}, u32[]{:S(2)}) collective-permute-start(f32[16,16,128]{2,1,0:T(8,128)S(1)} %get-tuple-element.37.after), channel_id=1, source_target_pairs={{0,6},{1,7},{2,4},{3,5},{4,2},{5,3},{6,0},{7,1},{8,14},{9,15},{10,... | collective-permute-start | bytes 393224 | tf_op jit(solution)/shard_map/ppermute | solution.py:364
  42.4 9.3 %product.5.refs_1_ = f32[256,1536]{1,0:T(8,128)S(1)} custom-call(s32[2]{0:T(128)S(1)} %pad_add_fusion.place, f32[16,16,128]{2,1,0:T(8,128)S(1)} %get-tuple-element.37.after, f32[4096,2048]{1,0:T(8,128)} %fisher.5, bf16[512,2048]{1,0:T(8,128)(2,1)S(1)} %get-tuple-element.31.queries), custom_call_target="tpu_custom_call" | custom-call | flops 4831838208 | bytes 12582912 | tf_op jit(solution)/shard_map/product/pallas_call | solution.py:263
  51.7 0.0 collective-permute-done.10.refs_2_
  51.7 0.0 collective-permute-done.11.refs_3_
  51.7 0.4 merge.1
  52.1 0.0 collective-permute-done.7
  52.2 0.0 collective-permute-done.8
  52.2 0.0 collective-permute-done.9
  52.2 2.1 %score.1 = f32[32,2,256]{2,1,0:T(2,128)} custom-call(s32[2]{0:T(128)S(1)} %pad_add_fusion.place, f32[256,128]{1,0:T(8,128)S(1)} %bitcast.8, f32[256,128]{1,0:T(8,128)S(1)} %bitcast.9, f32[256,128]{1,0:T(8,128)S(1)} %bitcast.10, f32[256,128]{1,0:T(8,128)S(1)} %bitcast.11, bf16[256,2048]{1,0:T(8,128)(2,1)S(1)} %get-tuple-element.39.refs_4_, ...), custom_call_target="tpu_custom_call" | custom-call | tf_op jit(solution)/shard_map/score/pallas_call | solution.py:331
  54.2 4.9 %all-to-all-start = ((f32[32,2,256]{2,1,0:T(2,128)}), f32[32,2,256]{2,1,0:T(2,128)S(1)}, u32[]{:S(2)}, u32[]{:S(2)}) async-start(f32[32,2,256]{2,1,0:T(2,128)} %score.1), calls=%async_computation | async-start | bytes 131072 | tf_op jit(solution)/shard_map/all_to_all | solution.py:387
  59.2 0.1 dynamic-slice_convert_fusion
  59.2 7.3 %all-to-all-done = f32[32,2,256]{2,1,0:T(2,128)S(1)} async-done(((f32[32,2,256]{2,1,0:T(2,128)}), f32[32,2,256]{2,1,0:T(2,128)S(1)}, u32[]{:S(2)}, u32[]{:S(2)}) %all-to-all-start) | async-done | bytes 65568 | tf_op jit(solution)/shard_map/all_to_all | solution.py:387
  66.6 0.7 multiply_divide_fusion
  (3 shorter events, 0.1 us)
Async XLA Ops:
  0.1 6.8 %copy-start.1 = (s32[64]{0:T(128)S(1)}, s32[64]{0:T(128)}, u32[]{:S(2)}) copy-start(s32[64]{0:T(128)} %offsets.1) | copy-start | bytes 772
  0.1 6.8 %copy-start.2 = (s32[64]{0:T(128)S(1)}, s32[64]{0:T(128)}, u32[]{:S(2)}) copy-start(s32[64]{0:T(128)} %lengths.1) | copy-start | bytes 772
  6.4 7.6 %copy-start = (f32[2048,256]{1,0:T(8,128)S(1)}, f32[2048,256]{1,0:T(8,128)}, u32[]{:S(2)}) copy-start(f32[2048,256]{1,0:T(8,128)} %queries.1) | copy-start | bytes 6291460
  6.4 1.6 %collective-permute-start = (f32[384,128]{1,0:T(8,128)S(1)}, f32[384,128]{1,0:T(8,128)S(1)}, u32[]{:S(2)}, u32[]{:S(2)}) collective-permute-start(f32[384,128]{1,0:T(8,128)S(1)} %get-tuple-element.24), channel_id=1, source_target_pairs={{0,1},{1,0},{2,3},{3,2},{4,5},{5,4},{6,7},{7,6},{8,9},{9,8},{10,11... | collective-permute-start | bytes 589832 | tf_op jit(solution)/shard_map/ppermute | solution.py:358
  9.5 11.7 %collective-permute-start.1 = (f32[17,16,128]{2,1,0:T(8,128)S(1)}, f32[17,16,128]{2,1,0:T(8,128)S(1)}, u32[]{:S(2)}, u32[]{:S(2)}) collective-permute-start(f32[17,16,128]{2,1,0:T(8,128)S(1)} %get-tuple-element.26), channel_id=1, source_target_pairs={{0,8},{8,0},{16,24},{24,16},{1,9},{9,1},{17,25},{25,17},{2,10},{10... | collective-permute-start | bytes 417800 | tf_op jit(solution)/shard_map/ppermute | solution.py:361
  12.4 8.8 %collective-permute-start.2 = (f32[17,16,128]{2,1,0:T(8,128)S(1)}, f32[17,16,128]{2,1,0:T(8,128)S(1)}, u32[]{:S(2)}, u32[]{:S(2)}) collective-permute-start(f32[17,16,128]{2,1,0:T(8,128)S(1)} %get-tuple-element.27), channel_id=1, source_target_pairs={{0,16},{8,24},{16,0},{24,8},{1,17},{9,25},{17,1},{25,9},{2,18},{10... | collective-permute-start | bytes 417800 | tf_op jit(solution)/shard_map/ppermute | solution.py:361
  13.9 7.3 %collective-permute-start.3 = (f32[17,16,128]{2,1,0:T(8,128)S(1)}, f32[17,16,128]{2,1,0:T(8,128)S(1)}, u32[]{:S(2)}, u32[]{:S(2)}) collective-permute-start(f32[17,16,128]{2,1,0:T(8,128)S(1)} %get-tuple-element.28), channel_id=1, source_target_pairs={{0,24},{8,16},{16,8},{24,0},{1,25},{9,17},{17,9},{25,1},{2,26},{10... | collective-permute-start | bytes 417800 | tf_op jit(solution)/shard_map/ppermute | solution.py:361
  21.1 30.6 %collective-permute-start.10 = (f32[256,1024]{1,0:T(8,128)S(1)}, f32[256,1024]{1,0:T(8,128)S(1)}, u32[]{:S(2)}, u32[]{:S(2)}) collective-permute-start(f32[256,1024]{1,0:T(8,128)S(1)} %get-tuple-element.29.refs_4_), channel_id=1, source_target_pairs={{0,1},{1,0},{2,3},{3,2},{4,5},{5,4},{6,7},{7,6},{8,9},{9,8},{10,11... | collective-permute-start | bytes 3145736 | tf_op jit(solution)/shard_map/ppermute | solution.py:358
  22.0 13.8 %collective-permute-start.4 = (f32[16,16,128]{2,1,0:T(8,128)S(1)}, f32[16,16,128]{2,1,0:T(8,128)S(1)}, u32[]{:S(2)}, u32[]{:S(2)}) collective-permute-start(f32[16,16,128]{2,1,0:T(8,128)S(1)} %get-tuple-element.34), channel_id=1, source_target_pairs={{0,6},{1,7},{2,4},{3,5},{4,2},{5,3},{6,0},{7,1},{8,14},{9,15},{10,... | collective-permute-start | bytes 393224 | tf_op jit(solution)/shard_map/ppermute | solution.py:364
  26.1 11.7 %collective-permute-start.5 = (f32[16,16,128]{2,1,0:T(8,128)S(1)}, f32[16,16,128]{2,1,0:T(8,128)S(1)}, u32[]{:S(2)}, u32[]{:S(2)}) collective-permute-start(f32[16,16,128]{2,1,0:T(8,128)S(1)} %get-tuple-element.35), channel_id=1, source_target_pairs={{0,4},{1,5},{2,6},{3,7},{4,0},{5,1},{6,2},{7,3},{8,12},{9,13},{10,... | collective-permute-start | bytes 393224 | tf_op jit(solution)/shard_map/ppermute | solution.py:364
  26.1 11.7 %collective-permute-start.6 = (f32[16,16,128]{2,1,0:T(8,128)S(1)}, f32[16,16,128]{2,1,0:T(8,128)S(1)}, u32[]{:S(2)}, u32[]{:S(2)}) collective-permute-start(f32[16,16,128]{2,1,0:T(8,128)S(1)} %get-tuple-element.36), channel_id=1, source_target_pairs={{0,2},{1,3},{2,0},{3,1},{4,6},{5,7},{6,4},{7,5},{8,10},{9,11},{10,... | collective-permute-start | bytes 393224 | tf_op jit(solution)/shard_map/ppermute | solution.py:364
  37.9 13.8 %collective-permute-start.11 = (f32[256,1024]{1,0:T(8,128)S(1)}, f32[256,1024]{1,0:T(8,128)S(1)}, u32[]{:S(2)}, u32[]{:S(2)}) collective-permute-start(f32[256,1024]{1,0:T(8,128)S(1)} %get-tuple-element.38), channel_id=1, source_target_pairs={{0,1},{1,0},{2,3},{3,2},{4,5},{5,4},{6,7},{7,6},{8,9},{9,8},{10,11... | collective-permute-start | bytes 3145736 | tf_op jit(solution)/shard_map/ppermute | solution.py:358
  38.0 14.2 %collective-permute-start.7 = (f32[16,16,128]{2,1,0:T(8,128)S(1)}, f32[16,16,128]{2,1,0:T(8,128)S(1)}, u32[]{:S(2)}, u32[]{:S(2)}) collective-permute-start(f32[16,16,128]{2,1,0:T(8,128)S(1)} %get-tuple-element.37.after), channel_id=1, source_target_pairs={{0,2},{1,3},{2,0},{3,1},{4,6},{5,7},{6,4},{7,5},{8,10},{9,11},{10,... | collective-permute-start | bytes 393224 | tf_op jit(solution)/shard_map/ppermute | solution.py:364
  38.0 14.1 %collective-permute-start.8 = (f32[16,16,128]{2,1,0:T(8,128)S(1)}, f32[16,16,128]{2,1,0:T(8,128)S(1)}, u32[]{:S(2)}, u32[]{:S(2)}) collective-permute-start(f32[16,16,128]{2,1,0:T(8,128)S(1)} %get-tuple-element.37.after), channel_id=1, source_target_pairs={{0,4},{1,5},{2,6},{3,7},{4,0},{5,1},{6,2},{7,3},{8,12},{9,13},{10,... | collective-permute-start | bytes 393224 | tf_op jit(solution)/shard_map/ppermute | solution.py:364
  41.1 11.1 %collective-permute-start.9 = (f32[16,16,128]{2,1,0:T(8,128)S(1)}, f32[16,16,128]{2,1,0:T(8,128)S(1)}, u32[]{:S(2)}, u32[]{:S(2)}) collective-permute-start(f32[16,16,128]{2,1,0:T(8,128)S(1)} %get-tuple-element.37.after), channel_id=1, source_target_pairs={{0,6},{1,7},{2,4},{3,5},{4,2},{5,3},{6,0},{7,1},{8,14},{9,15},{10,... | collective-permute-start | bytes 393224 | tf_op jit(solution)/shard_map/ppermute | solution.py:364
  54.2 12.3 %all-to-all-start = ((f32[32,2,256]{2,1,0:T(2,128)}), f32[32,2,256]{2,1,0:T(2,128)S(1)}, u32[]{:S(2)}, u32[]{:S(2)}) async-start(f32[32,2,256]{2,1,0:T(2,128)} %score.1), calls=%async_computation | async-start | bytes 131072 | tf_op jit(solution)/shard_map/all_to_all | solution.py:387

commit v3 on v2

v3 whole, which is shorter than its diff:
```python
import functools

import jax
import jax.numpy as jnp
from jax import lax
from jax.experimental import pallas as pl
from jax.experimental.pallas import tpu as pltpu
from jax.sharding import PartitionSpec as P

SHORTEST = 32
STEP = 256
MOST, LATER = 1, 64
CORES = 2
VMEM = pl.BlockSpec(memory_space=pltpu.VMEM)
SMEM = pl.BlockSpec(memory_space=pltpu.SMEM)
ANY = pl.BlockSpec(memory_space=pl.ANY)
HBM = pl.BlockSpec(memory_space=pltpu.HBM)

score_scale = 0.0625


def halves(x):
    high = x.astype(jnp.bfloat16)
    low = (x - high.astype(jnp.float32)).astype(jnp.bfloat16)
    return high, low


def dot(left, right):
    return jnp.dot(left, right, preferred_element_type=jnp.float32)


def params(mib):
    return pltpu.CompilerParams(vmem_limit_bytes=mib * 2**20)


def project_kernel(steps, row_count, place, hidden, grad, proj_in, proj_out, own, give, *scratch):
    hidden_v, grad_v, in_v, out_v, sems = scratch
    jobs = []
    for source, weights, left, right, count in (
        (grad, proj_out, grad_v, out_v, steps[0]),
        (hidden, proj_in, hidden_v, in_v, steps[1]),
    ):
        wide = source.shape[1] // count
        job = []
        for i in range(count):
            span = pl.ds(i * wide, wide)
            slot = len(jobs) * steps[0] + i
            a = pltpu.make_async_copy(source.at[:, span], left.at[:, span], sems.at[0, slot])
            b = pltpu.make_async_copy(weights.at[span, :], right.at[span, :], sems.at[1, slot])
            a.start()
            b.start()
            job.append((span, a, b))
        jobs.append((left, right, job))
    results = []
    for left, right, job in jobs:
        total = None
        for span, a, b in job:
            a.wait()
            b.wait()
            term = dot(left[:, span], right[span, :])
            total = term if total is None else total + term
        results.append(total)
    grads, tokens = results
    tok_rows, rank = tokens.shape
    band = rank // row_count // CORES
    turned = grads.T.reshape(row_count, CORES, band, tok_rows)
    first = turned[:, 0].reshape(row_count * band, tok_rows)
    second = turned[:, 1].reshape(row_count * band, tok_rows)
    mine = place[1] % CORES == 0
    tall = row_count * band
    for ref, value in ((own, jnp.where(mine, first, second)), (give, jnp.where(mine, second, first))):
        for i in range(tok_rows // rank):
            ref[i * tall : (i + 1) * tall, :] = value[:, i * rank : (i + 1) * rank]
        ref[tok_rows // rank * tall :, :] = tokens


def project(place, hidden_in, out_grad, proj_in, proj_out, row_count):
    tok_rows, rank = hidden_in.shape[0], proj_in.shape[1]
    steps = (2, 7)
    tall = tok_rows // rank * (rank // CORES) + tok_rows
    out = jax.ShapeDtypeStruct((tall, rank), jnp.float32)
    return pl.pallas_call(
        functools.partial(project_kernel, steps, row_count),
        out_shape=(out, out),
        in_specs=[SMEM, HBM, HBM, HBM, HBM],
        out_specs=(VMEM, VMEM),
        scratch_shapes=[
            pltpu.VMEM(hidden_in.shape, hidden_in.dtype),
            pltpu.VMEM(out_grad.shape, out_grad.dtype),
            pltpu.VMEM(proj_in.shape, proj_in.dtype),
            pltpu.VMEM(proj_out.shape, proj_out.dtype),
            pltpu.SemaphoreType.DMA((2, sum(steps))),
        ],
        compiler_params=params(53),
        name="project",
    )(place, hidden_in, out_grad, proj_in, proj_out)


def prepare_kernel(sizes, slots, after, offsets, lengths, queries, table, most, turned):
    row_count, col_count = sizes
    chips = row_count * col_count // CORES
    begin = lax.broadcasted_iota(jnp.int32, (chips, offsets.shape[1]), 0) * slots
    ended = (offsets[...] + lengths[...] <= begin).astype(jnp.int32).sum(axis=1, keepdims=True)
    begun = (offsets[...] < begin + slots).astype(jnp.int32).sum(axis=1, keepdims=True)
    lanes = lax.broadcasted_iota(jnp.int32, (chips, 2 * LATER), 1)
    met = jnp.sum((begun - ended).reshape(row_count, chips // row_count, 1), axis=0)
    most[0] = jnp.max(met)
    table[...] = jnp.where(lanes < LATER, jnp.where(lanes == MOST, jnp.max(met), ended), begun)
    high, low = halves(queries[...].T)
    width = high.shape[0]
    turned[:width, :] = high
    turned[width:, :] = low


def prepare(after, offsets, lengths, queries, sizes, tok_rows):
    depth, width = queries.shape
    chips = sizes[0] * sizes[1] // CORES
    return pl.pallas_call(
        functools.partial(prepare_kernel, sizes, CORES * tok_rows),
        out_shape=(
            jax.ShapeDtypeStruct((chips, 2 * LATER), jnp.int32),
            jax.ShapeDtypeStruct((1,), jnp.int32),
            jax.ShapeDtypeStruct((2 * width, depth), jnp.bfloat16),
        ),
        in_specs=[ANY, VMEM, VMEM, VMEM],
        out_specs=(VMEM, SMEM, VMEM),
        compiler_params=params(16),
        cost_estimate=pl.CostEstimate(flops=depth * width * 2048, bytes_accessed=8 * depth * width, transcendentals=0),
        name="prepare",
    )(after, offsets[None, :], lengths[None, :], queries)


def window_kernel(window, sizes, tok_rows, place, offsets, lengths, table, own, got, *refs):
    row_count, col_count = sizes
    outs, left = refs[:row_count], refs[row_count]
    device = place[0] * col_count + place[1]
    first_sample = jnp.minimum(table[device // CORES, 0], lengths.shape[0] - window)
    rank = own.shape[1]
    strips = tok_rows // rank
    tall = (own.shape[0] - tok_rows) // strips
    pieces = [ref[i * tall : (i + 1) * tall, :] for ref in (own, got) for i in range(strips)]
    grads_high, grads_low = halves(jnp.concatenate(pieces, axis=1))
    high, low = halves(jnp.concatenate([own[strips * tall :, :], got[strips * tall :, :]], axis=0))
    tokens = jnp.concatenate([high, low], axis=1)
    lanes = lax.broadcasted_iota(jnp.int32, (1, 2 * tok_rows), 1)
    other = device + 1 - 2 * (place[1] % CORES)
    positions = jnp.where(lanes < tok_rows, device * tok_rows + lanes, (other - 1) * tok_rows + lanes)
    both = jnp.concatenate([grads_high, grads_low], axis=0)
    for w in range(window):
        begin = offsets[first_sample + w]
        inside = (positions >= begin) & (positions < begin + lengths[first_sample + w])
        left[w * 2 * tall : (w + 1) * 2 * tall, :] = both * inside.astype(jnp.bfloat16)
    sums = dot(left[...], tokens)
    band = tall // row_count
    sums = sums.reshape(window, 2, row_count, band, 2 * rank)
    sums = sums[:, 0, :, :, :rank] + (sums[:, 0, :, :, rank:] + sums[:, 1, :, :, :rank])
    for r in range(row_count):
        step = place[0] ^ r
        for s in range(row_count):

            @pl.when(step == s)
            def _():
                outs[s][...] = sums[:, r]


def windows(place, offsets, lengths, table, own, got, window, sizes, tok_rows):
    rank = own.shape[1]
    tall = (own.shape[0] - tok_rows) // (tok_rows // rank)
    out = jax.ShapeDtypeStruct((window, tall // sizes[0], rank), jnp.float32)
    return pl.pallas_call(
        functools.partial(window_kernel, window, sizes, tok_rows),
        out_shape=(out,) * sizes[0],
        in_specs=[SMEM, SMEM, SMEM, SMEM, VMEM, VMEM],
        out_specs=(VMEM,) * sizes[0],
        scratch_shapes=[pltpu.VMEM((window * 2 * tall, 2 * tok_rows), jnp.bfloat16)],
        compiler_params=params(34),
        cost_estimate=pl.CostEstimate(
            flops=16 * window * tall * tok_rows * rank, bytes_accessed=8 * window * tall * rank, transcendentals=0
        ),
        name="windows",
    )(place, offsets, lengths, table, own, got)


def runs(place, table, sizes, step, samples, window):
    row_count, col_count = sizes
    chip, base, found = (place[1] // CORES) ^ step, 0, []
    for d in range(row_count):
        at = (place[0] ^ d) * (col_count // CORES) + chip
        first = table[at, 0]
        count = jnp.minimum(table[at, LATER] - first, window)
        found.append((first, count, first - jnp.minimum(first, samples - window), base))
        base = base + count
    return found


def pack_kernel(sizes, samples, cap, place, table, *refs):
    pieces, (first, rest, total) = refs[: sizes[0]], refs[sizes[0] + 1 :]
    window, band, rank = pieces[0].shape
    total[...] = jnp.zeros_like(total)
    for piece, (_, count, skip, base) in zip(pieces, runs(place, table, sizes, 0, samples, window)):

        def move(i, carry):
            total[base + i] = piece[skip + i]
            return carry

        lax.fori_loop(0, count, move, 0)
    rows = total.reshape(total.shape[0] * band, rank)
    for a in range(band):
        first[a * cap : (a + 1) * cap, :] = rows[pl.ds(a, cap, stride=band), :]
    for k in range(rest.shape[0]):

        @pl.when(table[0, MOST] > (k + 1) * cap)
        def _():
            for a in range(band):
                rest[k, a * cap : (a + 1) * cap, :] = rows[pl.ds((k + 1) * cap * band + a, cap, stride=band), :]


def pack(place, table, pieces, after, samples, cap, sizes):
    window, band, rank = pieces[0].shape
    rounds = -(-len(pieces) * window // cap)
    return pl.pallas_call(
        functools.partial(pack_kernel, sizes, samples, cap),
        out_shape=(
            jax.ShapeDtypeStruct((band * cap, rank), jnp.float32),
            jax.ShapeDtypeStruct((max(rounds - 1, 1), band * cap, rank), jnp.float32),
        ),
        in_specs=[SMEM, SMEM] + [VMEM] * len(pieces) + [ANY],
        out_specs=(VMEM, VMEM),
        scratch_shapes=[pltpu.VMEM((max(rounds, 2) * cap, band, rank), jnp.float32)],
        compiler_params=params(16),
        name="pack",
    )(place, table, *pieces, after)


def release_kernel(*refs):
    pass


def release(parts, after):
    return pl.pallas_call(
        release_kernel,
        out_shape=tuple(jax.ShapeDtypeStruct(part.shape, part.dtype) for part in parts),
        in_specs=[ANY] * (len(parts) + 1),
        out_specs=(ANY,) * len(parts),
        input_output_aliases={i + 1: i for i in range(len(parts))},
        compiler_params=params(16),
        name="release",
    )(after, *parts)


def across(left, right):
    return lax.dot_general(left, right, (((1,), (1,)), ((), ())), preferred_element_type=jnp.float32)


def rows_from(core, chunk, half):
    ours, first, _ = chunk
    return pl.multiple_of(jnp.where((core == 0) == ours, first, half + first), STEP)


def product_kernel(chunks, later, half, place, after, fisher, turned, *refs):
    count = len(chunks) + (1 if later else 0)
    heads, outs, (fisher_v, split, sems) = refs[: -3 - count], refs[-3 - count : -3], refs[-3:]
    core = place[1] % CORES
    ready = heads[0].shape[0] if heads else 0
    width = turned.shape[0] // 2
    copies, at = [], 0
    for chunk in chunks:
        source = rows_from(core, chunk, half)
        for step in range(0, chunk[2], STEP):
            if at >= ready:
                copy = pltpu.make_async_copy(
                    fisher.at[pl.ds(source + step, STEP), :],
                    fisher_v.at[pl.ds(at - ready, STEP), :],
                    sems.at[1 + at // STEP],
                )
                copy.start()
                copies.append(copy)
            else:
                copies.append(None)
            at += STEP
    if later:
        coming, outs = outs[0], outs[1:]
        source = rows_from(core, later, half)
        ahead = pltpu.make_async_copy(fisher.at[pl.ds(source, coming.shape[0]), :], coming, sems.at[0])
        ahead.start()
    at = 0
    for out, (_, _, rows) in zip(outs, chunks):
        for begin in range(0, rows, split.shape[1]):
            size = min(split.shape[1], rows - begin)
            for step in range(0, size, STEP):
                if copies[at // STEP] is None:
                    piece = heads[0][at : at + STEP, :]
                else:
                    copies[at // STEP].wait()
                    piece = fisher_v[at - ready : at - ready + STEP, :]
                split[0, step : step + STEP, :], split[1, step : step + STEP, :] = halves(piece)
                at += STEP
            term = across(turned[...], split[0, :size, :])
            term = term[:width] + (term[width:] + across(turned[:width, :], split[1, :size, :]))
            span = slice(begin, begin + size)
            out[:width, span], out[width:, span] = halves(term)
    if later:
        ahead.wait()


def product(place, after, inverse_fisher, head, turned, chunks, later=None):
    width = turned.shape[0] // 2
    heads = [] if head is None else [head]
    depth = inverse_fisher.shape[1]
    out_shape = [jax.ShapeDtypeStruct((2 * STEP, depth), jnp.float32)] if later else []
    out_shape += [jax.ShapeDtypeStruct((2 * width, chunk[2]), jnp.bfloat16) for chunk in chunks]
    rows = sum(chunk[2] for chunk in chunks)
    half = inverse_fisher.shape[0] // CORES
    return pl.pallas_call(
        functools.partial(product_kernel, chunks, later, half),
        out_shape=tuple(out_shape),
        in_specs=[SMEM, ANY, HBM, VMEM] + [VMEM] * len(heads),
        out_specs=(VMEM,) * len(out_shape),
        scratch_shapes=[
            pltpu.VMEM((rows - sum(h.shape[0] for h in heads), depth), jnp.float32),
            pltpu.VMEM((2, 2 * STEP, depth), jnp.bfloat16),
            pltpu.SemaphoreType.DMA((1 + rows // STEP,)),
        ],
        compiler_params=params(34),
        cost_estimate=pl.CostEstimate(
            flops=6 * rows * depth * width, bytes_accessed=4 * rows * depth, transcendentals=0
        ),
        name="product",
    )(place, after, inverse_fisher, turned, *heads)


def rows_times(parts, products, left, cap):
    rank = parts[0].shape[1]
    for i, part in enumerate(parts):
        for a in range(part.shape[0] // cap):
            left[i * cap : (i + 1) * cap, a * rank : (a + 1) * rank] = part[a * cap : (a + 1) * cap, :]
    slots = left.shape[0]
    total, at = None, 0
    for ref in products:
        width, depth = ref.shape[0] // 2, ref.shape[1]
        high, low = halves(left[:, at : at + depth])
        term = across(jnp.concatenate([high, low], axis=0), ref[:width, :])
        term = term[:slots] + (term[slots:] + across(high, ref[width:, :]))
        total = term if total is None else total + term
        at += depth
    return total


def own_score_kernel(count, cap, *refs):
    refs[-2][...] = rows_times(refs[:count], refs[count:-2], refs[-1], cap)


def own_score(parts, products, cap):
    depth = parts[0].shape[0] // cap * parts[0].shape[1]
    rows, width = len(parts) * cap, products[0].shape[0] // 2
    return pl.pallas_call(
        functools.partial(own_score_kernel, len(parts), cap),
        out_shape=jax.ShapeDtypeStruct((rows, width), jnp.float32),
        in_specs=[VMEM] * (len(parts) + len(products)),
        out_specs=VMEM,
        scratch_shapes=[pltpu.VMEM((rows, depth), jnp.float32)],
        compiler_params=params(16),
        cost_estimate=pl.CostEstimate(
            flops=64 * rows * depth * width, bytes_accessed=4 * depth * width, transcendentals=0
        ),
        name="own_score",
    )(*parts, *products)


def score_kernel(sizes, samples, window, cap, place, table, turn, own, *refs):
    chip_count = sizes[1] // CORES
    out, left = refs[-2:]
    total = own[...] + rows_times(refs[:chip_count], refs[chip_count:-2], left, cap)
    slots = chip_count * cap
    lanes = lax.broadcasted_iota(jnp.int32, (1, slots), 1)
    held = jnp.full((1, slots), -1, jnp.int32)
    for step in range(chip_count):
        at = lanes - step * cap
        here = (at >= 0) & (at < cap)
        at = at + turn[0] * cap
        for first, count, _, base in runs(place, table, sizes, step, samples, window):
            held = jnp.where(here & (at >= base) & (at < base + count), first + at - base, held)
    hit = lax.broadcasted_iota(jnp.int32, (samples, slots), 0) == held
    chosen = hit.astype(jnp.bfloat16)
    high, low = halves(total)
    out[...] = (dot(chosen, high) + dot(chosen, low)).reshape(out.shape)


def score(place, table, turn, own, parts, products, samples, window, cap, sizes):
    depth = parts[0].shape[0] // cap * parts[0].shape[1]
    width = products[0].shape[0] // 2
    devices = sizes[0] * sizes[1]
    return pl.pallas_call(
        functools.partial(score_kernel, sizes, samples, window, cap),
        out_shape=jax.ShapeDtypeStruct((devices, samples // devices, width), jnp.float32),
        in_specs=[SMEM, SMEM, SMEM] + [VMEM] * (1 + len(parts) + len(products)),
        out_specs=VMEM,
        scratch_shapes=[pltpu.VMEM((len(parts) * cap, depth), jnp.float32)],
        compiler_params=params(16),
        name="score",
    )(place, table, turn, own, *parts, *products)


def body(hidden_in, out_grad, proj_in, proj_out, inverse_fisher, queries, lengths, offsets):
    row_count = lax.axis_size("row")
    col_count = lax.axis_size("col")
    sizes = (row_count, col_count)
    chip_count = col_count // CORES
    row_id = lax.axis_index("row")
    col_id = lax.axis_index("col")
    tok_rows = hidden_in.shape[0]
    samples = lengths.shape[0]
    window = min(samples, CORES * tok_rows // SHORTEST + 1)
    cap = -(-3 * samples // (2 * chip_count))
    place = jnp.stack([row_id, col_id])

    def other_core(x):
        return lax.ppermute(x, "col", [(i, i ^ 1) for i in range(col_count)])

    def along_row(x, step):
        return lax.ppermute(x, "row", [(i, i ^ step) for i in range(row_count)])

    def along_col(x, step):
        return lax.ppermute(x, "col", [(i, i ^ (CORES * step)) for i in range(col_count)])

    own, give = project(place, hidden_in, out_grad, proj_in, proj_out, row_count)
    got = other_core(give)
    table, most, turned = prepare(give, offsets, lengths, queries, sizes, tok_rows)
    pieces = windows(place, offsets, lengths, table, own, got, window, sizes, tok_rows)

    half = inverse_fisher.shape[0] // CORES
    mid = half // 2
    chunks_a = [(True, 0, mid)]
    chunks_b = [(True, mid, mid), (False, 0, half)]
    arrived = [pieces[0]] + [along_row(pieces[d], d) for d in range(1, row_count)]
    head, *product_a = product(place, pieces[0], inverse_fisher, None, turned, chunks_a, chunks_b[0])
    packed, rest = pack(place, table, arrived, product_a[0], samples, cap, sizes)

    def everywhere(packed):
        return [packed] + [along_col(packed, d) for d in range(1, chip_count)]

    parts = everywhere(packed)
    product_b = product(place, packed, inverse_fisher, head, turned, chunks_b)
    products_own, products_other = [*product_a, product_b[0]], [product_b[1]]

    def terms_of(turn, parts):
        others = [other_core(part) for part in parts]
        turn = jnp.reshape(turn, (1,))
        own = own_score(parts, products_own, cap)
        return score(place, table, turn, own, others, products_other, samples, window, cap, sizes)

    score_terms = terms_of(jnp.int32(0), release(parts, product_b[0]))

    def another(state):
        turn, total = state
        packed = lax.dynamic_index_in_dim(rest, turn - 1, 0, False)
        return turn + 1, total + terms_of(turn, everywhere(packed))

    _, score_terms = lax.while_loop(lambda state: state[0] * cap < most[0], another, (jnp.int32(1), score_terms))
    devices = row_count * col_count

    terms = lax.all_to_all(score_terms, ("row", "col"), split_axis=0, concat_axis=0, tiled=True)
    owned_rows = samples // devices
    owned_scores = jnp.sum(terms, axis=0)
    device_id = row_id * col_count + col_id
    owned_lengths = lax.dynamic_slice_in_dim(lengths, device_id * owned_rows, owned_rows, 0)
    return score_scale * owned_scores / owned_lengths.astype(jnp.float32)[:, None]


def solution(mesh):
    in_specs = (
        P(("row", "col"), None),
        P(("row", "col"), None),
        P(),
        P(),
        P("row", "col"),
        P("col", None),
        P(),
        P(),
    )
    out_specs = P(("row", "col"), None)
    return jax.shard_map(body, mesh=mesh, in_specs=in_specs, out_specs=out_specs, check_vma=False)
```

time: 67.4 us -> 60.6 us (0.90)
  starting transfers between devices: 19.2 us -> 15.5 us
  Pallas kernels: 36.5 us -> 33.5 us
    ppermute x6 -> x3, starting transfers between devices: 9.2 us -> 4.79 us  [along_col(): lax.ppermute(x, 'col', [(i, i ^ CORES * step) for i in range(col_count)])]
    pallas_call x7, Pallas kernels: 28.7 us -> 25.6 us  [the longest x2 20.7 us: product(): pl.pallas_call(functools.partial(product_kernel, chunks, later, half), ou...]
    ppermute x3 -> x5, starting transfers between devices: 0.66 us -> 1.54 us  [other_core(): return lax.ppermute(x, 'col', [(i, i ^ 1) for i in range(col_count)])]
    ppermute x6 -> x3, waiting for transfers between devices: 2.04 us -> 1.74 us  [along_col(): lax.ppermute(x, 'col', [(i, i ^ CORES * step) for i in range(col_count)])]
  transfers between devices with their start and end apart: 13 -> 12, of which waited for: 3 -> 5; matrix products, arithmetic and copies ran while one was open for 0% -> 0% of each run, Pallas kernels for 40% -> 37%
where the time goes in v3:
time: 60.6 us; the launch traced here: 60.4 us
  Pallas kernels  33.5 us (55%)
  starting transfers between devices  15.5 us (26%)
  waiting for transfers between devices  9.82 us (16%)
  other arithmetic  0.85 us (1%)
    pallas_call x2, Pallas kernels, product(): pl.pallas_call(functools.partial(product_kernel, chunks, later, half), ou...  20.7 us
    all_to_all x1, waiting for transfers between devices, body(): lax.all_to_all(score_terms, ('row', 'col'), split_axis=0, concat_axis=0,...  7.3 us
    pallas_call x1, Pallas kernels, project(): pl.pallas_call(functools.partial(project_kernel, steps, row_count), out_s...  6.42 us
    ppermute x3, starting transfers between devices, along_col(): lax.ppermute(x, 'col', [(i, i ^ CORES * step) for i in range(col_count)])  4.79 us
    all_to_all x1, starting transfers between devices, body(): lax.all_to_all(score_terms, ('row', 'col'), split_axis=0, concat_axis=0,...  4.7 us
    ppermute x3, starting transfers between devices, along_row(): return lax.ppermute(x, 'row', [(i, i ^ step) for i in range(row_count)])  4.47 us
    pallas_call x1, Pallas kernels, score(): pl.pallas_call(functools.partial(score_kernel, sizes, samples, window, ca...  2.22 us
    ppermute x3, waiting for transfers between devices, along_col(): lax.ppermute(x, 'col', [(i, i ^ CORES * step) for i in range(col_count)])  1.74 us
  transfers between devices with their start and end apart: 12, of which 5 were waited for; matrix products, arithmetic and copies ran while one was open for 0% of the time, Pallas kernels for 37%

profile of v3, /device:TPU:0, one launch (start us, length us, event | category | flops | bytes accessed | tf_op | source)
XLA Modules:
  0.0 60.4 jit_solution(8557396708910788434)
XLA Ops:
  0.0 0.1 pad_add_fusion.place
  0.1 0.0 copy-start
  0.1 0.0 copy-start.1
  0.1 0.0 copy-start.2
  0.1 6.4 %project.1 = (f32[384,128]{1,0:T(8,128)S(1)}, f32[384,128]{1,0:T(8,128)S(1)}) custom-call(s32[2]{0:T(128)S(1)} %pad_add_fusion.place, bf16[256,14336]{1,0:T(8,128)(2,1)} %hidden.1, bf16[256,4096]{1,0:T(8,128)(2,1)} %grad.1, bf16[14336,128]{1,0:T(8,128)(2,1)} %proj_in.1, bf16[4096,128]{1,0:T(8,128)(2,1)} %proj_out.1), custom_call_target="tpu_custom_call" | custom-call | tf_op jit(solution)/shard_map/project/pallas_call | solution.py:82
  6.5 0.5 collective-permute-start.7
  7.0 0.0 copy-done
  7.0 0.0 copy-done.1
  7.0 0.0 copy-done.2
  7.0 0.7 %prepare.1 = (s32[16,128]{1,0:T(8,128)S(1)}, s32[1]{0:T(128)}, bf16[512,2048]{1,0:T(8,128)(2,1)S(1)}) custom-call(f32[384,128]{1,0:T(8,128)S(1)} %get-tuple-element.203.after, s32[1,64]{1,0:T(1,128)S(1)} %bitcast.13, s32[1,64]{1,0:T(1,128)S(1)} %bitcast.14, f32[2048,256]{1,0:T(8,128)S(1)} %copy-done), custom_call_target="tpu_custom_call" | custom-call | flops 1073741824 | bytes 4194304 | tf_op jit(solution)/shard_map/prepare/pallas_call | solution.py:118
  7.8 0.3 collective-permute-done.7.got
  8.1 1.5 %windows.1 = (f32[17,16,128]{2,1,0:T(8,128)S(1)}, f32[17,16,128]{2,1,0:T(8,128)S(1)}, f32[17,16,128]{2,1,0:T(8,128)S(1)}, f32[17,16,128]{2,1,0:T(8,128)S(1)}) custom-call(s32[2]{0:T(128)S(1)} %pad_add_fusion.place, s32[64]{0:T(128)S(1)} %copy-done.1, s32[64]{0:T(128)S(1)} %copy-done.2, s32[16,128]{1,0:T(8,128)S(1)} %get-tuple-element.304.table, ...), custom_call_target="tpu_custom_call" | custom-call | flops 570425344 | bytes 1114112 | tf_op jit(solution)/shard_map/windows/pallas_call | solution.py:170
  9.6 2.9 %collective-permute-start.8 = (f32[17,16,128]{2,1,0:T(8,128)S(1)}, f32[17,16,128]{2,1,0:T(8,128)S(1)}, u32[]{:S(2)}, u32[]{:S(2)}) collective-permute-start(f32[17,16,128]{2,1,0:T(8,128)S(1)} %get-tuple-element.207), channel_id=1, source_target_pairs={{0,8},{8,0},{16,24},{24,16},{1,9},{9,1},{17,25},{25,17},{2,10},{10... | collective-permute-start | bytes 417800 | tf_op jit(solution)/shard_map/ppermute | solution.py:421
  12.6 1.5 %collective-permute-start.9 = (f32[17,16,128]{2,1,0:T(8,128)S(1)}, f32[17,16,128]{2,1,0:T(8,128)S(1)}, u32[]{:S(2)}, u32[]{:S(2)}) collective-permute-start(f32[17,16,128]{2,1,0:T(8,128)S(1)} %get-tuple-element.208), channel_id=1, source_target_pairs={{0,16},{8,24},{16,0},{24,8},{1,17},{9,25},{17,1},{25,9},{2,18},{10... | collective-permute-start | bytes 417800 | tf_op jit(solution)/shard_map/ppermute | solution.py:421
  14.1 0.0 collective-permute-start.10
  14.1 7.0 %product.2 = (f32[512,2048]{1,0:T(8,128)S(1)}, bf16[512,1024]{1,0:T(8,128)(2,1)S(1)}) custom-call(s32[2]{0:T(128)S(1)} %pad_add_fusion.place, f32[17,16,128]{2,1,0:T(8,128)S(1)} %get-tuple-element.206.after.refs_0_, f32[4096,2048]{1,0:T(8,128)} %fisher.3, bf16[512,2048]{1,0:T(8,128)(2,1)S(1)} %get-tuple-element.210.turned), custom_call_target="tpu_custom_call" | custom-call | flops 3221225472 | bytes 8388608 | tf_op jit(solution)/shard_map/product/pallas_call | solution.py:314
  21.1 0.0 copy-start.3
  21.1 0.0 collective-permute-done.8.refs_1_
  21.1 0.0 collective-permute-done.9.refs_2_
  21.1 0.0 collective-permute-done.10.refs_3_
  21.1 1.1 %pack.1 = (f32[384,128]{1,0:T(8,128)S(1)}, f32[2,384,128]{2,1,0:T(8,128)S(1)}) custom-call(s32[2]{0:T(128)S(1)} %pad_add_fusion.place, s32[16,128]{1,0:T(8,128)S(1)} %get-tuple-element.304.table, f32[17,16,128]{2,1,0:T(8,128)S(1)} %get-tuple-element.206.after.refs_0_, f32[17,16,128]{2,1,0:T(8,128)S(1)} %collective-permute-done.8.refs_1_, ...), custom_call_target="tpu_custom_call" | custom-call | tf_op jit(solution)/shard_map/pack/pallas_call | solution.py:221
  22.2 4.1 %collective-permute-start.13 = (f32[384,128]{1,0:T(8,128)S(1)}, f32[384,128]{1,0:T(8,128)S(1)}, u32[]{:S(2)}, u32[]{:S(2)}) collective-permute-start(f32[384,128]{1,0:T(8,128)S(1)} %get-tuple-element.212.after.refs_1_), channel_id=1, source_target_pairs={{0,6},{1,7},{2,4},{3,5},{4,2},{5,3},{6,0},{7,1},{8,14},{9,15},{10,... | collective-permute-start | bytes 589832 | tf_op jit(solution)/shard_map/ppermute | solution.py:424
  26.3 0.0 collective-permute-start.12
  26.3 0.6 %collective-permute-start.11 = (f32[384,128]{1,0:T(8,128)S(1)}, f32[384,128]{1,0:T(8,128)S(1)}, u32[]{:S(2)}, u32[]{:S(2)}) collective-permute-start(f32[384,128]{1,0:T(8,128)S(1)} %get-tuple-element.212.after.refs_1_), channel_id=1, source_target_pairs={{0,2},{1,3},{2,0},{3,1},{4,6},{5,7},{6,4},{7,5},{8,10},{9,11},{10,... | collective-permute-start | bytes 589832 | tf_op jit(solution)/shard_map/ppermute | solution.py:424
  27.0 13.8 %product.3 = (bf16[512,1024]{1,0:T(8,128)(2,1)S(1)}, bf16[512,2048]{1,0:T(8,128)(2,1)S(1)}) custom-call(s32[2]{0:T(128)S(1)} %pad_add_fusion.place, f32[384,128]{1,0:T(8,128)S(1)} %get-tuple-element.212.after.refs_1_, f32[4096,2048]{1,0:T(8,128)} %fisher.3, bf16[512,2048]{1,0:T(8,128)(2,1)S(1)} %get-tuple-element.210.turned, ...), custom_call_target="tpu_custom_call" | custom-call | flops 9663676416 | bytes 25165824 | tf_op jit(solution)/shard_map/product/pallas_call | solution.py:314
  40.8 0.0 collective-permute-done.13.refs_4_
  40.8 1.7 %collective-permute-done.12.refs_3_ = f32[384,128]{1,0:T(8,128)S(1)} collective-permute-done((f32[384,128]{1,0:T(8,128)S(1)}, f32[384,128]{1,0:T(8,128)S(1)}, u32[]{:S(2)}, u32[]{:S(2)}) %collective-permute-start.12) | collective-permute-done | bytes 196640 | tf_op jit(solution)/shard_map/ppermute | solution.py:424
  42.5 0.0 collective-permute-done.11.refs_2_
  42.5 0.0 collective-permute-start.14
  42.5 0.5 collective-permute-start.15
  43.0 0.1 collective-permute-start.16
  43.1 0.4 collective-permute-start.17
  43.5 0.0 copy-done.3
  43.5 0.8 %own_score.2.own = f32[96,256]{1,0:T(8,128)S(1)} custom-call(f32[384,128]{1,0:T(8,128)S(1)} %get-tuple-element.215.refs_0_, f32[384,128]{1,0:T(8,128)S(1)} %get-tuple-element.216.refs_1_, f32[384,128]{1,0:T(8,128)S(1)} %get-tuple-element.217.refs_2_, f32[384,128]{1,0:T(8,128)S(1)} %get-tuple-element.218.refs_3_, ...), custom_call_target="tpu_custom_call" | custom-call | flops 3221225472 | bytes 2097152 | tf_op jit(solution)/shard_map/own_score/pallas_call | solution.py:356
  44.4 0.0 collective-permute-done.14.refs_0_
  44.4 0.0 collective-permute-done.15.refs_1_
  44.4 0.1 collective-permute-done.16.refs_2_
  44.5 0.3 collective-permute-done.17.refs_3_
  44.8 2.2 %score.8 = f32[32,2,256]{2,1,0:T(2,128)} custom-call(s32[2]{0:T(128)S(1)} %pad_add_fusion.place, s32[16,128]{1,0:T(8,128)S(1)} %get-tuple-element.304.table, s32[1]{0:T(128)} %constant.53.clone.1.turn, f32[96,256]{1,0:T(8,128)S(1)} %own_score.2.own, f32[384,128]{1,0:T(8,128)S(1)} %collective-permute-done.14.refs_0_, ...), custom_call_target="tpu_custom_call" | custom-call | tf_op jit(solution)/shard_map/score/pallas_call | solution.py:393
  47.0 0.6 while.14
  47.6 4.7 %all-to-all-start = ((f32[32,2,256]{2,1,0:T(2,128)}), f32[32,2,256]{2,1,0:T(2,128)S(1)}, u32[]{:S(2)}, u32[]{:S(2)}) async-start(f32[32,2,256]{2,1,0:T(2,128)} %get-tuple-element.222), calls=%async_computation | async-start | bytes 131072 | tf_op jit(solution)/shard_map/all_to_all | solution.py:462
  52.3 0.1 dynamic-slice_convert_fusion
  52.4 7.3 %all-to-all-done = f32[32,2,256]{2,1,0:T(2,128)S(1)} async-done(((f32[32,2,256]{2,1,0:T(2,128)}), f32[32,2,256]{2,1,0:T(2,128)S(1)}, u32[]{:S(2)}, u32[]{:S(2)}) %all-to-all-start) | async-done | bytes 65568 | tf_op jit(solution)/shard_map/all_to_all | solution.py:462
  59.7 0.7 %multiply_divide_fusion = f32[2,256]{1,0:T(2,128)} fusion(f32[2,256]{1,0:T(2,128)S(1)} %reduce_sum.9, f32[2]{0:T(128)S(1)} %dynamic-slice_convert_fusion), kind=kLoop, calls=%fused_computation.1 | loop fusion | flops 1024 | bytes 4104 | tf_op jit(solution)/shard_map/div | solution.py:467
  (2 shorter events, 0.0 us)
Async XLA Ops:
  0.1 7.0 %copy-start = (f32[2048,256]{1,0:T(8,128)S(1)}, f32[2048,256]{1,0:T(8,128)}, u32[]{:S(2)}) copy-start(f32[2048,256]{1,0:T(8,128)} %queries.1) | copy-start | bytes 6291460
  0.1 7.0 %copy-start.1 = (s32[64]{0:T(128)S(1)}, s32[64]{0:T(128)}, u32[]{:S(2)}) copy-start(s32[64]{0:T(128)} %offsets.1) | copy-start | bytes 772
  0.1 7.0 %copy-start.2 = (s32[64]{0:T(128)S(1)}, s32[64]{0:T(128)}, u32[]{:S(2)}) copy-start(s32[64]{0:T(128)} %lengths.1) | copy-start | bytes 772
  6.5 1.6 %collective-permute-start.7 = (f32[384,128]{1,0:T(8,128)S(1)}, f32[384,128]{1,0:T(8,128)S(1)}, u32[]{:S(2)}, u32[]{:S(2)}) collective-permute-start(f32[384,128]{1,0:T(8,128)S(1)} %get-tuple-element.203.after), channel_id=1, source_target_pairs={{0,1},{1,0},{2,3},{3,2},{4,5},{5,4},{6,7},{7,6},{8,9},{9,8},{10,11... | collective-permute-start | bytes 589832 | tf_op jit(solution)/shard_map/ppermute | solution.py:418
  9.6 11.4 %collective-permute-start.8 = (f32[17,16,128]{2,1,0:T(8,128)S(1)}, f32[17,16,128]{2,1,0:T(8,128)S(1)}, u32[]{:S(2)}, u32[]{:S(2)}) collective-permute-start(f32[17,16,128]{2,1,0:T(8,128)S(1)} %get-tuple-element.207), channel_id=1, source_target_pairs={{0,8},{8,0},{16,24},{24,16},{1,9},{9,1},{17,25},{25,17},{2,10},{10... | collective-permute-start | bytes 417800 | tf_op jit(solution)/shard_map/ppermute | solution.py:421
  12.6 8.5 %collective-permute-start.9 = (f32[17,16,128]{2,1,0:T(8,128)S(1)}, f32[17,16,128]{2,1,0:T(8,128)S(1)}, u32[]{:S(2)}, u32[]{:S(2)}) collective-permute-start(f32[17,16,128]{2,1,0:T(8,128)S(1)} %get-tuple-element.208), channel_id=1, source_target_pairs={{0,16},{8,24},{16,0},{24,8},{1,17},{9,25},{17,1},{25,9},{2,18},{10... | collective-permute-start | bytes 417800 | tf_op jit(solution)/shard_map/ppermute | solution.py:421
  14.1 7.0 %collective-permute-start.10 = (f32[17,16,128]{2,1,0:T(8,128)S(1)}, f32[17,16,128]{2,1,0:T(8,128)S(1)}, u32[]{:S(2)}, u32[]{:S(2)}) collective-permute-start(f32[17,16,128]{2,1,0:T(8,128)S(1)} %get-tuple-element.209), channel_id=1, source_target_pairs={{0,24},{8,16},{16,8},{24,0},{1,25},{9,17},{17,9},{25,1},{2,26},{10... | collective-permute-start | bytes 417800 | tf_op jit(solution)/shard_map/ppermute | solution.py:421
  21.1 22.5 %copy-start.3 = (bf16[512,1024]{1,0:T(8,128)(2,1)}, bf16[512,1024]{1,0:T(8,128)(2,1)S(1)}, u32[]{:S(2)}) copy-start(bf16[512,1024]{1,0:T(8,128)(2,1)S(1)} %get-tuple-element.301.refs_4_) | copy-start | bytes 3145732
  22.2 18.6 %collective-permute-start.13 = (f32[384,128]{1,0:T(8,128)S(1)}, f32[384,128]{1,0:T(8,128)S(1)}, u32[]{:S(2)}, u32[]{:S(2)}) collective-permute-start(f32[384,128]{1,0:T(8,128)S(1)} %get-tuple-element.212.after.refs_1_), channel_id=1, source_target_pairs={{0,6},{1,7},{2,4},{3,5},{4,2},{5,3},{6,0},{7,1},{8,14},{9,15},{10,... | collective-permute-start | bytes 589832 | tf_op jit(solution)/shard_map/ppermute | solution.py:424
  26.3 16.2 %collective-permute-start.12 = (f32[384,128]{1,0:T(8,128)S(1)}, f32[384,128]{1,0:T(8,128)S(1)}, u32[]{:S(2)}, u32[]{:S(2)}) collective-permute-start(f32[384,128]{1,0:T(8,128)S(1)} %get-tuple-element.212.after.refs_1_), channel_id=1, source_target_pairs={{0,4},{1,5},{2,6},{3,7},{4,0},{5,1},{6,2},{7,3},{8,12},{9,13},{10,... | collective-permute-start | bytes 589832 | tf_op jit(solution)/shard_map/ppermute | solution.py:424
  26.3 16.2 %collective-permute-start.11 = (f32[384,128]{1,0:T(8,128)S(1)}, f32[384,128]{1,0:T(8,128)S(1)}, u32[]{:S(2)}, u32[]{:S(2)}) collective-permute-start(f32[384,128]{1,0:T(8,128)S(1)} %get-tuple-element.212.after.refs_1_), channel_id=1, source_target_pairs={{0,2},{1,3},{2,0},{3,1},{4,6},{5,7},{6,4},{7,5},{8,10},{9,11},{10,... | collective-permute-start | bytes 589832 | tf_op jit(solution)/shard_map/ppermute | solution.py:424
  42.5 1.8 %collective-permute-start.14 = (f32[384,128]{1,0:T(8,128)S(1)}, f32[384,128]{1,0:T(8,128)S(1)}, u32[]{:S(2)}, u32[]{:S(2)}) collective-permute-start(f32[384,128]{1,0:T(8,128)S(1)} %get-tuple-element.215.refs_0_), channel_id=1, source_target_pairs={{0,1},{1,0},{2,3},{3,2},{4,5},{5,4},{6,7},{7,6},{8,9},{9,8},{10,11... | collective-permute-start | bytes 589832 | tf_op jit(solution)/shard_map/ppermute | solution.py:418
  42.5 1.8 %collective-permute-start.15 = (f32[384,128]{1,0:T(8,128)S(1)}, f32[384,128]{1,0:T(8,128)S(1)}, u32[]{:S(2)}, u32[]{:S(2)}) collective-permute-start(f32[384,128]{1,0:T(8,128)S(1)} %get-tuple-element.216.refs_1_), channel_id=1, source_target_pairs={{0,1},{1,0},{2,3},{3,2},{4,5},{5,4},{6,7},{7,6},{8,9},{9,8},{10,11... | collective-permute-start | bytes 589832 | tf_op jit(solution)/shard_map/ppermute | solution.py:418
  43.0 1.5 %collective-permute-start.16 = (f32[384,128]{1,0:T(8,128)S(1)}, f32[384,128]{1,0:T(8,128)S(1)}, u32[]{:S(2)}, u32[]{:S(2)}) collective-permute-start(f32[384,128]{1,0:T(8,128)S(1)} %get-tuple-element.217.refs_2_), channel_id=1, source_target_pairs={{0,1},{1,0},{2,3},{3,2},{4,5},{5,4},{6,7},{7,6},{8,9},{9,8},{10,11... | collective-permute-start | bytes 589832 | tf_op jit(solution)/shard_map/ppermute | solution.py:418
  43.1 1.7 %collective-permute-start.17 = (f32[384,128]{1,0:T(8,128)S(1)}, f32[384,128]{1,0:T(8,128)S(1)}, u32[]{:S(2)}, u32[]{:S(2)}) collective-permute-start(f32[384,128]{1,0:T(8,128)S(1)} %get-tuple-element.218.refs_3_), channel_id=1, source_target_pairs={{0,1},{1,0},{2,3},{3,2},{4,5},{5,4},{6,7},{7,6},{8,9},{9,8},{10,11... | collective-permute-start | bytes 589832 | tf_op jit(solution)/shard_map/ppermute | solution.py:418
  47.6 12.1 %all-to-all-start = ((f32[32,2,256]{2,1,0:T(2,128)}), f32[32,2,256]{2,1,0:T(2,128)S(1)}, u32[]{:S(2)}, u32[]{:S(2)}) async-start(f32[32,2,256]{2,1,0:T(2,128)} %get-tuple-element.222), calls=%async_computation | async-start | bytes 131072 | tf_op jit(solution)/shard_map/all_to_all | solution.py:462

commit v4 on v3

--- a/solution.py
+++ b/solution.py
@@ -51,7 +51,10 @@
             b.start()
             job.append((span, a, b))
         jobs.append((left, right, job))
-    results = []
+    tok_rows, rank = hidden.shape[0], proj_in.shape[1]
+    band = rank // row_count // CORES
+    tall = row_count * band
+    mine = place[1] % CORES == 0
     for left, right, job in jobs:
         total = None
         for span, a, b in job:
@@ -59,19 +62,16 @@
             b.wait()
             term = dot(left[:, span], right[span, :])
             total = term if total is None else total + term
-        results.append(total)
-    grads, tokens = results
-    tok_rows, rank = tokens.shape
-    band = rank // row_count // CORES
-    turned = grads.T.reshape(row_count, CORES, band, tok_rows)
-    first = turned[:, 0].reshape(row_count * band, tok_rows)
-    second = turned[:, 1].reshape(row_count * band, tok_rows)
-    mine = place[1] % CORES == 0
-    tall = row_count * band
-    for ref, value in ((own, jnp.where(mine, first, second)), (give, jnp.where(mine, second, first))):
-        for i in range(tok_rows // rank):
-            ref[i * tall : (i + 1) * tall, :] = value[:, i * rank : (i + 1) * rank]
-        ref[tok_rows // rank * tall :, :] = tokens
+        if left is grad_v:
+            turned = total.T.reshape(row_count, CORES, band, tok_rows)
+            first = turned[:, 0].reshape(tall, tok_rows)
+            second = turned[:, 1].reshape(tall, tok_rows)
+            for ref, value in ((own, jnp.where(mine, first, second)), (give, jnp.where(mine, second, first))):
+                for i in range(tok_rows // rank):
+                    ref[i * tall : (i + 1) * tall, :] = value[:, i * rank : (i + 1) * rank]
+        else:
+            own[tok_rows // rank * tall :, :] = total
+            give[tok_rows // rank * tall :, :] = total
 
 
 def project(place, hidden_in, out_grad, proj_in, proj_out, row_count):
@@ -94,6 +94,11 @@
         compiler_params=params(53),
         name="project",
     )(place, hidden_in, out_grad, proj_in, proj_out)
+
+
+def rows_from(core, chunk, half):
+    ours, first, _ = chunk
+    return pl.multiple_of(jnp.where((core == 0) == ours, first, half + first), STEP)
 
 
 def prepare_kernel(sizes, slots, after, offsets, lengths, queries, table, most, turned):
@@ -252,16 +257,12 @@
     return lax.dot_general(left, right, (((1,), (1,)), ((), ())), preferred_element_type=jnp.float32)
 
 
-def rows_from(core, chunk, half):
-    ours, first, _ = chunk
-    return pl.multiple_of(jnp.where((core == 0) == ours, first, half + first), STEP)
-
-
 def product_kernel(chunks, later, half, place, after, fisher, turned, *refs):
     count = len(chunks) + (1 if later else 0)
     heads, outs, (fisher_v, split, sems) = refs[: -3 - count], refs[-3 - count : -3], refs[-3:]
     core = place[1] % CORES
-    ready = heads[0].shape[0] if heads else 0
+    early = [ref.at[pl.ds(i, STEP), :] for ref in heads for i in range(0, ref.shape[0], STEP)]
+    ready = len(early) * STEP
     width = turned.shape[0] // 2
     copies, at = [], 0
     for chunk in chunks:
@@ -289,7 +290,7 @@
             size = min(split.shape[1], rows - begin)
             for step in range(0, size, STEP):
                 if copies[at // STEP] is None:
-                    piece = heads[0][at : at + STEP, :]
+                    piece = early[at // STEP][...]
                 else:
                     copies[at // STEP].wait()
                     piece = fisher_v[at - ready : at - ready + STEP, :]
@@ -303,9 +304,8 @@
         ahead.wait()
 
 
-def product(place, after, inverse_fisher, head, turned, chunks, later=None):
+def product(place, after, inverse_fisher, heads, turned, chunks, later=None):
     width = turned.shape[0] // 2
-    heads = [] if head is None else [head]
     depth = inverse_fisher.shape[1]
     out_shape = [jax.ShapeDtypeStruct((2 * STEP, depth), jnp.float32)] if later else []
     out_shape += [jax.ShapeDtypeStruct((2 * width, chunk[2]), jnp.bfloat16) for chunk in chunks]
@@ -346,31 +346,10 @@
     return total
 
 
-def own_score_kernel(count, cap, *refs):
-    refs[-2][...] = rows_times(refs[:count], refs[count:-2], refs[-1], cap)
-
-
-def own_score(parts, products, cap):
-    depth = parts[0].shape[0] // cap * parts[0].shape[1]
-    rows, width = len(parts) * cap, products[0].shape[0] // 2
-    return pl.pallas_call(
-        functools.partial(own_score_kernel, len(parts), cap),
-        out_shape=jax.ShapeDtypeStruct((rows, width), jnp.float32),
-        in_specs=[VMEM] * (len(parts) + len(products)),
-        out_specs=VMEM,
-        scratch_shapes=[pltpu.VMEM((rows, depth), jnp.float32)],
-        compiler_params=params(16),
-        cost_estimate=pl.CostEstimate(
-            flops=64 * rows * depth * width, bytes_accessed=4 * depth * width, transcendentals=0
-        ),
-        name="own_score",
-    )(*parts, *products)
-
-
-def score_kernel(sizes, samples, window, cap, place, table, turn, own, *refs):
+def own_score_kernel(sizes, samples, window, cap, place, table, turn, *refs):
     chip_count = sizes[1] // CORES
-    out, left = refs[-2:]
-    total = own[...] + rows_times(refs[:chip_count], refs[chip_count:-2], left, cap)
+    out, out_held, left = refs[-3:]
+    out[...] = rows_times(refs[:chip_count], refs[chip_count:-3], left, cap)
     slots = chip_count * cap
     lanes = lax.broadcasted_iota(jnp.int32, (1, slots), 1)
     held = jnp.full((1, slots), -1, jnp.int32)
@@ -380,25 +359,49 @@
         at = at + turn[0] * cap
         for first, count, _, base in runs(place, table, sizes, step, samples, window):
             held = jnp.where(here & (at >= base) & (at < base + count), first + at - base, held)
-    hit = lax.broadcasted_iota(jnp.int32, (samples, slots), 0) == held
+    out_held[...] = jnp.broadcast_to(held, out_held.shape)
+
+
+def own_score(place, table, turn, parts, products, samples, window, cap, sizes):
+    depth = parts[0].shape[0] // cap * parts[0].shape[1]
+    rows, width = len(parts) * cap, products[0].shape[0] // 2
+    return pl.pallas_call(
+        functools.partial(own_score_kernel, sizes, samples, window, cap),
+        out_shape=(jax.ShapeDtypeStruct((rows, width), jnp.float32), jax.ShapeDtypeStruct((8, rows), jnp.int32)),
+        in_specs=[SMEM, SMEM, SMEM] + [VMEM] * (len(parts) + len(products)),
+        out_specs=(VMEM, VMEM),
+        scratch_shapes=[pltpu.VMEM((rows, depth), jnp.float32)],
+        compiler_params=params(16),
+        cost_estimate=pl.CostEstimate(
+            flops=64 * rows * depth * width, bytes_accessed=4 * depth * width, transcendentals=0
+        ),
+        name="own_score",
+    )(place, table, turn, *parts, *products)
+
+
+def score_kernel(chip_count, samples, cap, own, held, *refs):
+    out, left = refs[-2:]
+    total = own[...] + rows_times(refs[:chip_count], refs[chip_count:-2], left, cap)
+    slots = chip_count * cap
+    hit = lax.broadcasted_iota(jnp.int32, (samples, slots), 0) == held[:1, :]
     chosen = hit.astype(jnp.bfloat16)
     high, low = halves(total)
     out[...] = (dot(chosen, high) + dot(chosen, low)).reshape(out.shape)
 
 
-def score(place, table, turn, own, parts, products, samples, window, cap, sizes):
+def score(own, held, parts, products, samples, cap, sizes):
     depth = parts[0].shape[0] // cap * parts[0].shape[1]
     width = products[0].shape[0] // 2
     devices = sizes[0] * sizes[1]
     return pl.pallas_call(
-        functools.partial(score_kernel, sizes, samples, window, cap),
+        functools.partial(score_kernel, len(parts), samples, cap),
         out_shape=jax.ShapeDtypeStruct((devices, samples // devices, width), jnp.float32),
-        in_specs=[SMEM, SMEM, SMEM] + [VMEM] * (1 + len(parts) + len(products)),
+        in_specs=[VMEM] * (2 + len(parts) + len(products)),
         out_specs=VMEM,
         scratch_shapes=[pltpu.VMEM((len(parts) * cap, depth), jnp.float32)],
         compiler_params=params(16),
         name="score",
-    )(place, table, turn, own, *parts, *products)
+    )(own, held, *parts, *products)
 
 
 def body(hidden_in, out_grad, proj_in, proj_out, inverse_fisher, queries, lengths, offsets):
@@ -425,36 +428,37 @@
 
     own, give = project(place, hidden_in, out_grad, proj_in, proj_out, row_count)
     got = other_core(give)
-    table, most, turned = prepare(give, offsets, lengths, queries, sizes, tok_rows)
-    pieces = windows(place, offsets, lengths, table, own, got, window, sizes, tok_rows)
-
     half = inverse_fisher.shape[0] // CORES
     mid = half // 2
     chunks_a = [(True, 0, mid)]
     chunks_b = [(True, mid, mid), (False, 0, half)]
+    table, most, turned = prepare(give, offsets, lengths, queries, sizes, tok_rows)
+    pieces = windows(place, offsets, lengths, table, own, got, window, sizes, tok_rows)
+
     arrived = [pieces[0]] + [along_row(pieces[d], d) for d in range(1, row_count)]
-    head, *product_a = product(place, pieces[0], inverse_fisher, None, turned, chunks_a, chunks_b[0])
+    head, *product_a = product(place, pieces[0], inverse_fisher, [], turned, chunks_a, chunks_b[0])
     packed, rest = pack(place, table, arrived, product_a[0], samples, cap, sizes)
 
     def everywhere(packed):
         return [packed] + [along_col(packed, d) for d in range(1, chip_count)]
 
     parts = everywhere(packed)
-    product_b = product(place, packed, inverse_fisher, head, turned, chunks_b)
+    product_b = product(place, packed, inverse_fisher, [head], turned, chunks_b)
     products_own, products_other = [*product_a, product_b[0]], [product_b[1]]
 
-    def terms_of(turn, parts):
-        others = [other_core(part) for part in parts]
+    def terms_of(turn, parts, other):
+        others = [other] + [other_core(part) for part in parts[1:]]
         turn = jnp.reshape(turn, (1,))
-        own = own_score(parts, products_own, cap)
-        return score(place, table, turn, own, others, products_other, samples, window, cap, sizes)
-
-    score_terms = terms_of(jnp.int32(0), release(parts, product_b[0]))
+        own, held = own_score(place, table, turn, parts, products_own, samples, window, cap, sizes)
+        return score(own, held, others, products_other, samples, cap, sizes)
+
+    parts = release(parts, product_b[0])
+    score_terms = terms_of(jnp.int32(0), parts, other_core(parts[0]))
 
     def another(state):
         turn, total = state
         packed = lax.dynamic_index_in_dim(rest, turn - 1, 0, False)
-        return turn + 1, total + terms_of(turn, everywhere(packed))
+        return turn + 1, total + terms_of(turn, everywhere(packed), other_core(packed))
 
     _, score_terms = lax.while_loop(lambda state: state[0] * cap < most[0], another, (jnp.int32(1), score_terms))
     devices = row_count * col_count

time: 60.6 us -> 60.2 us (level)
  transfers between devices with their start and end apart: 12 -> 12, of which waited for: 5 -> 3; matrix products, arithmetic and copies ran while one was open for 0% -> 0% of each run, Pallas kernels for 37% -> 37%
where the time goes in v4:
time: 60.2 us; the launch traced here: 60 us
  Pallas kernels  33.1 us (55%)
  starting transfers between devices  15.5 us (26%)
  waiting for transfers between devices  9.72 us (16%)
  other arithmetic  0.85 us (1%)
  loops' own time  0.7 us (1%)
    pallas_call x2, Pallas kernels, product(): pl.pallas_call(functools.partial(product_kernel, chunks, later, half), ou...  20.3 us
    all_to_all x1, waiting for transfers between devices, body(): lax.all_to_all(score_terms, ('row', 'col'), split_axis=0, concat_axis=0,...  7.3 us
    pallas_call x1, Pallas kernels, project(): pl.pallas_call(functools.partial(project_kernel, steps, row_count), out_s...  6.42 us
    ppermute x3, starting transfers between devices, along_col(): lax.ppermute(x, 'col', [(i, i ^ CORES * step) for i in range(col_count)])  4.77 us
    all_to_all x1, starting transfers between devices, body(): lax.all_to_all(score_terms, ('row', 'col'), split_axis=0, concat_axis=0,...  4.72 us
    ppermute x3, starting transfers between devices, along_row(): return lax.ppermute(x, 'row', [(i, i ^ step) for i in range(row_count)])  4.47 us
    ppermute x3, waiting for transfers between devices, along_col(): lax.ppermute(x, 'col', [(i, i ^ CORES * step) for i in range(col_count)])  2.05 us
    pallas_call x1, Pallas kernels, score(): pl.pallas_call(functools.partial(score_kernel, len(parts), samples, cap),...  1.57 us
  transfers between devices with their start and end apart: 12, of which 3 were waited for; matrix products, arithmetic and copies ran while one was open for 0% of the time, Pallas kernels for 37%

profile of v4, /device:TPU:0, one launch (start us, length us, event | category | flops | bytes accessed | tf_op | source)
XLA Modules:
  0.0 60.0 jit_solution(11079447109025262952)
XLA Ops:
  0.0 0.1 pad_add_fusion.place
  0.1 0.0 copy-start
  0.1 0.0 copy-start.1
  0.1 0.0 copy-start.2
  0.1 6.4 %project.1 = (f32[384,128]{1,0:T(8,128)S(1)}, f32[384,128]{1,0:T(8,128)S(1)}) custom-call(s32[2]{0:T(128)S(1)} %pad_add_fusion.place, bf16[256,14336]{1,0:T(8,128)(2,1)} %hidden.1, bf16[256,4096]{1,0:T(8,128)(2,1)} %grad.1, bf16[14336,128]{1,0:T(8,128)(2,1)} %proj_in.1, bf16[4096,128]{1,0:T(8,128)(2,1)} %proj_out.1), custom_call_target="tpu_custom_call" | custom-call | tf_op jit(solution)/shard_map/project/pallas_call | solution.py:82
  6.5 0.5 collective-permute-start.7
  7.0 0.0 copy-done
  7.0 0.0 copy-done.1
  7.0 0.0 copy-done.2
  7.0 0.7 %prepare.1 = (s32[16,128]{1,0:T(8,128)S(1)}, s32[1]{0:T(128)}, bf16[512,2048]{1,0:T(8,128)(2,1)S(1)}) custom-call(f32[384,128]{1,0:T(8,128)S(1)} %get-tuple-element.207.after, s32[1,64]{1,0:T(1,128)S(1)} %bitcast.13, s32[1,64]{1,0:T(1,128)S(1)} %bitcast.14, f32[2048,256]{1,0:T(8,128)S(1)} %copy-done), custom_call_target="tpu_custom_call" | custom-call | flops 1073741824 | bytes 4194304 | tf_op jit(solution)/shard_map/prepare/pallas_call | solution.py:123
  7.8 0.3 collective-permute-done.7.got
  8.1 1.5 %windows.1 = (f32[17,16,128]{2,1,0:T(8,128)S(1)}, f32[17,16,128]{2,1,0:T(8,128)S(1)}, f32[17,16,128]{2,1,0:T(8,128)S(1)}, f32[17,16,128]{2,1,0:T(8,128)S(1)}) custom-call(s32[2]{0:T(128)S(1)} %pad_add_fusion.place, s32[64]{0:T(128)S(1)} %copy-done.1, s32[64]{0:T(128)S(1)} %copy-done.2, s32[16,128]{1,0:T(8,128)S(1)} %get-tuple-element.312.table, ...), custom_call_target="tpu_custom_call" | custom-call | flops 570425344 | bytes 1114112 | tf_op jit(solution)/shard_map/windows/pallas_call | solution.py:175
  9.6 2.9 %collective-permute-start.8 = (f32[17,16,128]{2,1,0:T(8,128)S(1)}, f32[17,16,128]{2,1,0:T(8,128)S(1)}, u32[]{:S(2)}, u32[]{:S(2)}) collective-permute-start(f32[17,16,128]{2,1,0:T(8,128)S(1)} %get-tuple-element.211), channel_id=1, source_target_pairs={{0,8},{8,0},{16,24},{24,16},{1,9},{9,1},{17,25},{25,17},{2,10},{10... | collective-permute-start | bytes 417800 | tf_op jit(solution)/shard_map/ppermute | solution.py:424
  12.6 1.5 %collective-permute-start.9 = (f32[17,16,128]{2,1,0:T(8,128)S(1)}, f32[17,16,128]{2,1,0:T(8,128)S(1)}, u32[]{:S(2)}, u32[]{:S(2)}) collective-permute-start(f32[17,16,128]{2,1,0:T(8,128)S(1)} %get-tuple-element.212), channel_id=1, source_target_pairs={{0,16},{8,24},{16,0},{24,8},{1,17},{9,25},{17,1},{25,9},{2,18},{10... | collective-permute-start | bytes 417800 | tf_op jit(solution)/shard_map/ppermute | solution.py:424
  14.1 0.0 collective-permute-start.10
  14.1 6.8 %product.2 = (f32[512,2048]{1,0:T(8,128)S(1)}, bf16[512,1024]{1,0:T(8,128)(2,1)S(1)}) custom-call(s32[2]{0:T(128)S(1)} %pad_add_fusion.place, f32[17,16,128]{2,1,0:T(8,128)S(1)} %get-tuple-element.210.after.refs_0_, f32[4096,2048]{1,0:T(8,128)} %fisher.3, bf16[512,2048]{1,0:T(8,128)(2,1)S(1)} %get-tuple-element.214.turned), custom_call_target="tpu_custom_call" | custom-call | flops 3221225472 | bytes 8388608 | tf_op jit(solution)/shard_map/product/pallas_call | solution.py:314
  20.9 0.0 copy-start.4
  21.0 0.0 collective-permute-done.8.refs_1_
  21.0 0.0 collective-permute-done.9.refs_2_
  21.0 0.0 collective-permute-done.10.refs_3_
  21.0 1.1 %pack.1 = (f32[384,128]{1,0:T(8,128)S(1)}, f32[2,384,128]{2,1,0:T(8,128)S(1)}) custom-call(s32[2]{0:T(128)S(1)} %pad_add_fusion.place, s32[16,128]{1,0:T(8,128)S(1)} %get-tuple-element.312.table, f32[17,16,128]{2,1,0:T(8,128)S(1)} %get-tuple-element.210.after.refs_0_, f32[17,16,128]{2,1,0:T(8,128)S(1)} %collective-permute-done.8.refs_1_, ...), custom_call_target="tpu_custom_call" | custom-call | tf_op jit(solution)/shard_map/pack/pallas_call | solution.py:226
  22.1 4.1 %collective-permute-start.13 = (f32[384,128]{1,0:T(8,128)S(1)}, f32[384,128]{1,0:T(8,128)S(1)}, u32[]{:S(2)}, u32[]{:S(2)}) collective-permute-start(f32[384,128]{1,0:T(8,128)S(1)} %get-tuple-element.216.after.refs_1_), channel_id=1, source_target_pairs={{0,6},{1,7},{2,4},{3,5},{4,2},{5,3},{6,0},{7,1},{8,14},{9,15},{10,... | collective-permute-start | bytes 589832 | tf_op jit(solution)/shard_map/ppermute | solution.py:427
  26.2 0.0 collective-permute-start.12
  26.2 0.6 %collective-permute-start.11 = (f32[384,128]{1,0:T(8,128)S(1)}, f32[384,128]{1,0:T(8,128)S(1)}, u32[]{:S(2)}, u32[]{:S(2)}) collective-permute-start(f32[384,128]{1,0:T(8,128)S(1)} %get-tuple-element.216.after.refs_1_), channel_id=1, source_target_pairs={{0,2},{1,3},{2,0},{3,1},{4,6},{5,7},{6,4},{7,5},{8,10},{9,11},{10,... | collective-permute-start | bytes 589832 | tf_op jit(solution)/shard_map/ppermute | solution.py:427
  26.9 13.5 %product.3 = (bf16[512,1024]{1,0:T(8,128)(2,1)S(1)}, bf16[512,2048]{1,0:T(8,128)(2,1)S(1)}) custom-call(s32[2]{0:T(128)S(1)} %pad_add_fusion.place, f32[384,128]{1,0:T(8,128)S(1)} %get-tuple-element.216.after.refs_1_, f32[4096,2048]{1,0:T(8,128)} %fisher.3, bf16[512,2048]{1,0:T(8,128)(2,1)S(1)} %get-tuple-element.214.turned, ...), custom_call_target="tpu_custom_call" | custom-call | flops 9663676416 | bytes 25165824 | tf_op jit(solution)/shard_map/product/pallas_call | solution.py:314
  40.3 0.0 copy-start.3
  40.3 0.0 collective-permute-done.13.refs_4_
  40.3 2.0 %collective-permute-done.12.refs_3_ = f32[384,128]{1,0:T(8,128)S(1)} collective-permute-done((f32[384,128]{1,0:T(8,128)S(1)}, f32[384,128]{1,0:T(8,128)S(1)}, u32[]{:S(2)}, u32[]{:S(2)}) %collective-permute-start.12) | collective-permute-done | bytes 196640 | tf_op jit(solution)/shard_map/ppermute | solution.py:427
  42.4 0.0 collective-permute-done.11.refs_2_
  42.4 0.0 collective-permute-start.14
  42.4 0.5 collective-permute-start.15
  42.9 0.1 collective-permute-start.16
  43.0 0.4 collective-permute-start.17
  43.4 0.0 copy-done.4
  43.4 1.5 %own_score.8 = (f32[96,256]{1,0:T(8,128)S(1)}, s32[8,96]{1,0:T(8,128)S(1)}) custom-call(s32[2]{0:T(128)S(1)} %pad_add_fusion.place, s32[16,128]{1,0:T(8,128)S(1)} %get-tuple-element.312.table, s32[1]{0:T(128)} %constant.53.clone.1.turn, f32[384,128]{1,0:T(8,128)S(1)} %get-tuple-element.219.refs_0_, f32[384,128]{1,0:T(8,128)S(1)} %get-tuple-element.220.refs_1_, ...), custom_call_target="tpu_custom_call" | custom-call | flops 3221225472 | bytes 2097152 | tf_op jit(solution)/shard_map/own_score/pallas_call | solution.py:368
  44.9 0.0 collective-permute-done.14.refs_0_
  44.9 0.0 collective-permute-done.15.refs_1_
  44.9 0.0 collective-permute-done.16.refs_2_
  44.9 0.0 collective-permute-done.17.refs_3_
  44.9 1.6 %score.8 = f32[32,2,256]{2,1,0:T(2,128)} custom-call(f32[96,256]{1,0:T(8,128)S(1)} %get-tuple-element.223.own, s32[8,96]{1,0:T(8,128)S(1)} %get-tuple-element.224.held, f32[384,128]{1,0:T(8,128)S(1)} %collective-permute-done.14.refs_0_, f32[384,128]{1,0:T(8,128)S(1)} %collective-permute-done.15.refs_1_, f32[384,128]{1,0:T(8,128)S(1)} %collective-permute-done.16.refs_2_, ...), custom_call_target="tpu_custom_call" | custom-call | tf_op jit(solution)/shard_map/score/pallas_call | solution.py:396
  46.5 0.0 copy-done.3
  46.5 0.7 %while.14 = (s32[]{:T(128)}, f32[32,2,256]{2,1,0:T(2,128)}, s32[1]{0:T(128)}, f32[2,384,128]{2,1,0:T(8,128)S(1)}, s32[2]{0:T(128)S(1)}, /*index=5*/s32[16,128]{1...) while((s32[]{:T(128)}, f32[32,2,256]{2,1,0:T(2,128)}, ...), condition=%wide.region_1.2_spmd, body=%wide.region_0.1_spmd.sunk | while | flops 3221241856 | bytes 8192455 | solution.py:463
  47.2 4.7 %all-to-all-start = ((f32[32,2,256]{2,1,0:T(2,128)}), f32[32,2,256]{2,1,0:T(2,128)S(1)}, u32[]{:S(2)}, u32[]{:S(2)}) async-start(f32[32,2,256]{2,1,0:T(2,128)} %get-tuple-element.228), calls=%async_computation | async-start | bytes 131072 | tf_op jit(solution)/shard_map/all_to_all | solution.py:466
  51.9 0.1 dynamic-slice_convert_fusion
  52.0 7.3 %all-to-all-done = f32[32,2,256]{2,1,0:T(2,128)S(1)} async-done(((f32[32,2,256]{2,1,0:T(2,128)}), f32[32,2,256]{2,1,0:T(2,128)S(1)}, u32[]{:S(2)}, u32[]{:S(2)}) %all-to-all-start) | async-done | bytes 65568 | tf_op jit(solution)/shard_map/all_to_all | solution.py:466
  59.4 0.7 %multiply_divide_fusion = f32[2,256]{1,0:T(2,128)} fusion(f32[2,256]{1,0:T(2,128)S(1)} %reduce_sum.9, f32[2]{0:T(128)S(1)} %dynamic-slice_convert_fusion), kind=kLoop, calls=%fused_computation.1 | loop fusion | flops 1024 | bytes 4104 | tf_op jit(solution)/shard_map/div | solution.py:471
  (2 shorter events, 0.0 us)
Async XLA Ops:
  0.1 7.0 %copy-start = (f32[2048,256]{1,0:T(8,128)S(1)}, f32[2048,256]{1,0:T(8,128)}, u32[]{:S(2)}) copy-start(f32[2048,256]{1,0:T(8,128)} %queries.1) | copy-start | bytes 6291460
  0.1 7.0 %copy-start.1 = (s32[64]{0:T(128)S(1)}, s32[64]{0:T(128)}, u32[]{:S(2)}) copy-start(s32[64]{0:T(128)} %offsets.1) | copy-start | bytes 772
  0.1 7.0 %copy-start.2 = (s32[64]{0:T(128)S(1)}, s32[64]{0:T(128)}, u32[]{:S(2)}) copy-start(s32[64]{0:T(128)} %lengths.1) | copy-start | bytes 772
  6.5 1.6 %collective-permute-start.7 = (f32[384,128]{1,0:T(8,128)S(1)}, f32[384,128]{1,0:T(8,128)S(1)}, u32[]{:S(2)}, u32[]{:S(2)}) collective-permute-start(f32[384,128]{1,0:T(8,128)S(1)} %get-tuple-element.207.after), channel_id=1, source_target_pairs={{0,1},{1,0},{2,3},{3,2},{4,5},{5,4},{6,7},{7,6},{8,9},{9,8},{10,11... | collective-permute-start | bytes 589832 | tf_op jit(solution)/shard_map/ppermute | solution.py:421
  9.6 11.3 %collective-permute-start.8 = (f32[17,16,128]{2,1,0:T(8,128)S(1)}, f32[17,16,128]{2,1,0:T(8,128)S(1)}, u32[]{:S(2)}, u32[]{:S(2)}) collective-permute-start(f32[17,16,128]{2,1,0:T(8,128)S(1)} %get-tuple-element.211), channel_id=1, source_target_pairs={{0,8},{8,0},{16,24},{24,16},{1,9},{9,1},{17,25},{25,17},{2,10},{10... | collective-permute-start | bytes 417800 | tf_op jit(solution)/shard_map/ppermute | solution.py:424
  12.6 8.4 %collective-permute-start.9 = (f32[17,16,128]{2,1,0:T(8,128)S(1)}, f32[17,16,128]{2,1,0:T(8,128)S(1)}, u32[]{:S(2)}, u32[]{:S(2)}) collective-permute-start(f32[17,16,128]{2,1,0:T(8,128)S(1)} %get-tuple-element.212), channel_id=1, source_target_pairs={{0,16},{8,24},{16,0},{24,8},{1,17},{9,25},{17,1},{25,9},{2,18},{10... | collective-permute-start | bytes 417800 | tf_op jit(solution)/shard_map/ppermute | solution.py:424
  14.1 6.9 %collective-permute-start.10 = (f32[17,16,128]{2,1,0:T(8,128)S(1)}, f32[17,16,128]{2,1,0:T(8,128)S(1)}, u32[]{:S(2)}, u32[]{:S(2)}) collective-permute-start(f32[17,16,128]{2,1,0:T(8,128)S(1)} %get-tuple-element.213), channel_id=1, source_target_pairs={{0,24},{8,16},{16,8},{24,0},{1,25},{9,17},{17,9},{25,1},{2,26},{10... | collective-permute-start | bytes 417800 | tf_op jit(solution)/shard_map/ppermute | solution.py:424
  20.9 22.5 %copy-start.4 = (bf16[512,1024]{1,0:T(8,128)(2,1)}, bf16[512,1024]{1,0:T(8,128)(2,1)S(1)}, u32[]{:S(2)}) copy-start(bf16[512,1024]{1,0:T(8,128)(2,1)S(1)} %get-tuple-element.313.refs_4_) | copy-start | bytes 3145732
  22.1 18.2 %collective-permute-start.13 = (f32[384,128]{1,0:T(8,128)S(1)}, f32[384,128]{1,0:T(8,128)S(1)}, u32[]{:S(2)}, u32[]{:S(2)}) collective-permute-start(f32[384,128]{1,0:T(8,128)S(1)} %get-tuple-element.216.after.refs_1_), channel_id=1, source_target_pairs={{0,6},{1,7},{2,4},{3,5},{4,2},{5,3},{6,0},{7,1},{8,14},{9,15},{10,... | collective-permute-start | bytes 589832 | tf_op jit(solution)/shard_map/ppermute | solution.py:427
  26.2 16.2 %collective-permute-start.12 = (f32[384,128]{1,0:T(8,128)S(1)}, f32[384,128]{1,0:T(8,128)S(1)}, u32[]{:S(2)}, u32[]{:S(2)}) collective-permute-start(f32[384,128]{1,0:T(8,128)S(1)} %get-tuple-element.216.after.refs_1_), channel_id=1, source_target_pairs={{0,4},{1,5},{2,6},{3,7},{4,0},{5,1},{6,2},{7,3},{8,12},{9,13},{10,... | collective-permute-start | bytes 589832 | tf_op jit(solution)/shard_map/ppermute | solution.py:427
  26.2 16.2 %collective-permute-start.11 = (f32[384,128]{1,0:T(8,128)S(1)}, f32[384,128]{1,0:T(8,128)S(1)}, u32[]{:S(2)}, u32[]{:S(2)}) collective-permute-start(f32[384,128]{1,0:T(8,128)S(1)} %get-tuple-element.216.after.refs_1_), channel_id=1, source_target_pairs={{0,2},{1,3},{2,0},{3,1},{4,6},{5,7},{6,4},{7,5},{8,10},{9,11},{10,... | collective-permute-start | bytes 589832 | tf_op jit(solution)/shard_map/ppermute | solution.py:427
  40.3 6.2 %copy-start.3 = (bf16[512,1024]{1,0:T(8,128)(2,1)}, bf16[512,1024]{1,0:T(8,128)(2,1)S(1)}, u32[]{:S(2)}) copy-start(bf16[512,1024]{1,0:T(8,128)(2,1)S(1)} %get-tuple-element.314.refs_0_.refs_5_) | copy-start | bytes 3145732
  42.4 2.5 %collective-permute-start.14 = (f32[384,128]{1,0:T(8,128)S(1)}, f32[384,128]{1,0:T(8,128)S(1)}, u32[]{:S(2)}, u32[]{:S(2)}) collective-permute-start(f32[384,128]{1,0:T(8,128)S(1)} %get-tuple-element.219.refs_0_), channel_id=1, source_target_pairs={{0,1},{1,0},{2,3},{3,2},{4,5},{5,4},{6,7},{7,6},{8,9},{9,8},{10,11... | collective-permute-start | bytes 589832 | tf_op jit(solution)/shard_map/ppermute | solution.py:421
  42.4 2.5 %collective-permute-start.15 = (f32[384,128]{1,0:T(8,128)S(1)}, f32[384,128]{1,0:T(8,128)S(1)}, u32[]{:S(2)}, u32[]{:S(2)}) collective-permute-start(f32[384,128]{1,0:T(8,128)S(1)} %get-tuple-element.220.refs_1_), channel_id=1, source_target_pairs={{0,1},{1,0},{2,3},{3,2},{4,5},{5,4},{6,7},{7,6},{8,9},{9,8},{10,11... | collective-permute-start | bytes 589832 | tf_op jit(solution)/shard_map/ppermute | solution.py:421
  42.9 2.0 %collective-permute-start.16 = (f32[384,128]{1,0:T(8,128)S(1)}, f32[384,128]{1,0:T(8,128)S(1)}, u32[]{:S(2)}, u32[]{:S(2)}) collective-permute-start(f32[384,128]{1,0:T(8,128)S(1)} %get-tuple-element.221.refs_2_), channel_id=1, source_target_pairs={{0,1},{1,0},{2,3},{3,2},{4,5},{5,4},{6,7},{7,6},{8,9},{9,8},{10,11... | collective-permute-start | bytes 589832 | tf_op jit(solution)/shard_map/ppermute | solution.py:421
  43.0 2.0 %collective-permute-start.17 = (f32[384,128]{1,0:T(8,128)S(1)}, f32[384,128]{1,0:T(8,128)S(1)}, u32[]{:S(2)}, u32[]{:S(2)}) collective-permute-start(f32[384,128]{1,0:T(8,128)S(1)} %get-tuple-element.222.refs_3_), channel_id=1, source_target_pairs={{0,1},{1,0},{2,3},{3,2},{4,5},{5,4},{6,7},{7,6},{8,9},{9,8},{10,11... | collective-permute-start | bytes 589832 | tf_op jit(solution)/shard_map/ppermute | solution.py:421
  47.2 12.1 %all-to-all-start = ((f32[32,2,256]{2,1,0:T(2,128)}), f32[32,2,256]{2,1,0:T(2,128)S(1)}, u32[]{:S(2)}, u32[]{:S(2)}) async-start(f32[32,2,256]{2,1,0:T(2,128)} %get-tuple-element.228), calls=%async_computation | async-start | bytes 131072 | tf_op jit(solution)/shard_map/all_to_all | solution.py:466
